TPU v7x, 512 devices: a whole 4x8x8 slice. The times are simulated.
512 devices in a mesh: dp: 32 (over z, y_hi, core), space: 16 (over y_lo, x).
Axes of the slice: x: 4, y: 8 (y_hi: 2, y_lo: 4; y = y_hi * 4 + y_lo), z: 8, core: 2. Of those that a mesh axis runs over, the one named last changes fastest.
Arguments:
- state: bfloat16 [32, 16, 32, 32, 256], P('dp', 'space'), may hold values from -6 to 6
- cotangent: bfloat16 [32, 16, 32, 32, 256], P('dp', 'space'), may hold values from -0.01953125 to 0.01953125
- kernel: bfloat16 [49, 256], replicated, may hold values from -0.875 to 0.875
- ln_gain: float32 [256], replicated, may hold values from 0.5 to 1.5
- w_in: bfloat16 [256, 1024], replicated, may hold values from -0.375 to 0.375
- w_out: bfloat16 [1024, 256], replicated, may hold values from -0.1875 to 0.1875
- layer_scale: float32 [256], replicated, may hold values from 0.5 to 1.5
- neighbours: int32 [16, 8], replicated, may hold values from -1 to 15, as said below
- codes: int32 [16, 8], replicated, may hold values from 0 to 3
Outputs:
- kernel_grad: float32 [49, 256], replicated
- gain_grad: float32 [256], replicated
- scale_grad: float32 [256], replicated
- in_grad: bfloat16 [256, 1024], replicated
- out_grad: bfloat16 [1024, 256], replicated
Inputs may be any that keep to these rules, and one draw needn't show every extreme that they name: `neighbours`: slots 0 to 3 name the tiles across a tile's sides clockwise from the top, slots 4 to 7 those across its corners, corner q lying between sides q - 1 and q; -1 marks a corner with no tile, which happens only in slots 4 to 7.
All inputs are finite; a program needn't handle non-finite values.
Results may differ from a plain program's by a relative error of at most 0.0072.
Values may be sent and summed in bfloat16 or wider, within the bound.
A program may use at most 64 MiB of HBM per device.

v0:
```python
import jax
import jax.numpy as jnp
from jax import lax
from jax.sharding import PartitionSpec as P

EPSILON = 1e-06


def as_sent(value):

    def short(part):
        return part.astype(jnp.bfloat16) if part.dtype == jnp.float32 else part

    return jax.tree.map(short, value)


def side_strips(tile):
    return jnp.stack([jnp.rot90(tile, turn, axes=(0, 1))[:3] for turn in range(4)])


def build_frame(tile, pieces, blocks):
    frame = jnp.pad(tile, ((3, 3), (3, 3), (0, 0)))
    for turn in range(4):
        turned = jnp.rot90(frame, turn, axes=(0, 1))
        turned = turned.at[0:3, 3:-3].set(pieces[turn]).at[0:3, 0:3].set(blocks[turn])
        frame = jnp.rot90(turned, -turn, axes=(0, 1))
    return frame


def facing_pieces(strips_all, tile_ids, tile_codes):
    present = tile_ids >= 0
    picked = strips_all[jnp.maximum(tile_ids, 0), tile_codes]
    pieces = picked[:, :4, ::-1, ::-1]
    corner = picked[:, 4:, :, :3][:, :, ::-1, ::-1]
    blocks = jnp.where(present[:, 4:, None, None, None], corner, jnp.zeros_like(corner))
    return (pieces, blocks)


def inner_rows(left, right):
    return lax.dot_general(
        left, right, (((0,), (0,)), ((), ())), preferred_element_type=jnp.float32
    )


def inner_cols(left, right):
    return lax.dot_general(
        left, right, (((1,), (1,)), ((), ())), preferred_element_type=jnp.float32
    )


def gelu_tanh(value):
    return jax.nn.gelu(value, approximate=True)


def block_grads(tiles, frames, cotan, kernel, ln_gain, w_in, w_out, layer_scale):
    side = tiles.shape[1]
    width = tiles.shape[3]
    depthwise = jnp.zeros(tiles.shape, jnp.float32)
    for offset in range(49):
        row_at, col_at = (offset // 7, offset % 7)
        window = frames[:, row_at : row_at + side, col_at : col_at + side].astype(jnp.float32)
        depthwise = depthwise + window * kernel[offset].astype(jnp.float32)
    flat = depthwise.reshape(-1, width)
    centered = flat - jnp.mean(flat, axis=-1, keepdims=True)
    inverse = lax.rsqrt(jnp.mean(centered * centered, axis=-1, keepdims=True) + EPSILON)
    normed = centered * inverse
    scaled = (normed * ln_gain).astype(jnp.bfloat16)
    pre_act = jnp.dot(scaled, w_in, preferred_element_type=jnp.float32)
    hidden = gelu_tanh(pre_act).astype(jnp.bfloat16)
    output = jnp.dot(hidden, w_out, preferred_element_type=jnp.float32)
    upstream = cotan.reshape(-1, width).astype(jnp.float32)
    scale_grad = jnp.sum(upstream * output, axis=0)
    branch = (upstream * layer_scale).astype(jnp.bfloat16)
    out_grad = inner_rows(hidden, branch)
    hidden_grad = inner_cols(branch, w_out)
    _, pullback = jax.vjp(gelu_tanh, pre_act)
    pre_grad = pullback(hidden_grad)[0].astype(jnp.bfloat16)
    in_grad = inner_rows(scaled, pre_grad)
    scaled_grad = inner_cols(pre_grad, w_in)
    gain_grad = jnp.sum(scaled_grad * normed, axis=0)
    normed_grad = scaled_grad * ln_gain
    depth_grad = (
        normed_grad
        - jnp.mean(normed_grad, axis=-1, keepdims=True)
        - normed * jnp.mean(normed_grad * normed, axis=-1, keepdims=True)
    ) * inverse
    depth_grad = depth_grad.reshape(tiles.shape)
    kernel_rows = []
    for offset in range(49):
        row_at, col_at = (offset // 7, offset % 7)
        window = frames[:, row_at : row_at + side, col_at : col_at + side].astype(jnp.float32)
        kernel_rows.append(jnp.sum(depth_grad * window, axis=(0, 1, 2)))
    return (jnp.stack(kernel_rows), gain_grad, scale_grad, in_grad, out_grad)


def on_device(state, cotangent, kernel, ln_gain, w_in, w_out, layer_scale, neighbours, codes):
    tiles = state[0]
    cotan = cotangent[0]
    count = tiles.shape[0]
    strips = jax.vmap(side_strips)(tiles)
    strips_all = jax.tree.map(
        lambda part, own: part.astype(own.dtype),
        lax.all_gather(as_sent(strips), "space", axis=0, tiled=True),
        strips,
    )
    first_tile = lax.axis_index("space") * count
    tile_ids = lax.dynamic_slice_in_dim(neighbours, first_tile, count, 0)
    tile_codes = lax.dynamic_slice_in_dim(codes, first_tile, count, 0)
    pieces, blocks = facing_pieces(strips_all, tile_ids, tile_codes)
    frames = jax.vmap(build_frame)(tiles, pieces, blocks)
    kernel_grad, gain_grad, scale_grad, in_grad, out_grad = block_grads(
        tiles, frames, cotan, kernel, ln_gain, w_in, w_out, layer_scale
    )
    kernel_grad, gain_grad, scale_grad, in_grad, out_grad = lax.psum(
        (kernel_grad, gain_grad, scale_grad, in_grad, out_grad), ("dp", "space")
    )
    in_grad = in_grad.astype(jnp.bfloat16)
    out_grad = out_grad.astype(jnp.bfloat16)
    return (kernel_grad, gain_grad, scale_grad, in_grad, out_grad)


def solution(mesh):
    placed = (
        P("dp", "space", None, None, None),
        P("dp", "space", None, None, None),
        P(),
        P(),
        P(),
        P(),
        P(),
        P(),
        P(),
    )
    return jax.shard_map(
        on_device, mesh=mesh, in_specs=placed, out_specs=(P(), P(), P(), P(), P()), check_vma=False
    )
```

profile of v0, /device:TPU:1, one launch (start us, length us, event | category | flops | bytes accessed | tf_op | source)
XLA Modules:
  0.0 280.7 jit_solution(8796577825602494266)
XLA Ops:
  7.2 0.0 copy-start
  7.2 0.0 copy-start.7
  7.2 0.0 all-gather.3.cloned.1.call-start
  7.3 1.4 copy.255
  8.7 0.1 slice_bitcast_fusion
  8.8 0.1 slice.663
  8.9 0.2 slice.661
  9.1 0.7 pad_maximum_fusion
  9.8 0.0 all-gather.3.cloned.1.call-update
  9.9 0.4 pad.36
  10.3 0.2 fusion.110
  10.5 0.1 dynamic-slice_compare_fusion
  10.6 0.6 fusion.114
  11.2 0.1 slice_reduce_fusion
  11.4 0.7 and_reduce_fusion
  12.1 0.6 slice_convert_fusion.46
  12.7 0.7 slice_convert_fusion.48
  13.4 0.7 slice_convert_fusion.47
  14.1 81.3 %all-gather.3.cloned.1.call-done = bf16[64,1,3,32,256]{4,3,2,1,0:T(8,128)(2,1)} async-done(((bf16[4,1,3,32,256]{4,3,2,1,0:T(8,128)(2,1)}), bf16[64,1,3,32,256]{4,3,2,1,0:T(8,128)(2,1)}) %all-gather.3.cloned.1.call-update) | async-done | bytes 3145744 | tf_op jit(solution)/shard_map/all_gather | solution.py:103
  95.4 2.5 gather_fusion
  97.9 0.1 rev.45
  98.0 0.1 broadcast_select_fusion
  98.2 0.2 slice.665
  98.4 2.0 bitcast_select_fusion.1
  100.5 1.7 scatter.26
  102.1 0.2 scatter.29
  102.3 0.1 reverse_bitcast_fusion.1
  102.4 0.1 rev.46
  102.4 0.7 slice.678
  103.1 0.1 slice.672
  103.3 0.2 slice.675
  103.5 1.9 bitcast_select_fusion.3
  105.4 1.5 scatter.30
  107.0 0.2 scatter.31
  107.2 1.9 rev.47
  109.1 2.0 bitcast_select_fusion
  111.1 1.7 scatter.34
  112.7 0.2 scatter.35
  112.9 1.9 rev.48
  114.8 1.9 rev.49
  116.7 1.9 bitcast_select_fusion.2
  118.7 1.5 scatter.36
  120.2 0.2 scatter.39
  120.4 1.9 rev.50
  122.3 9.4 %fusion.111 = (f32[32,32]{0,1:T(8,128)S(1)}, f32[1,32,32,256]{3,1,2,0:T(8,128)S(1)}) fusion(f32[256]{0:T(256)} %bitcast.247, bf16[1,38,38,256]{3,1,2,0:T(8,128)(2,1)S(1)} %bitcast.170, f32[256]{0:T(256)} %bitcast.248, f32[256]{0:T(256)} %bitcast.250, f32[256]{0:T(256)} %bitcast.251, f32[256]{0:T(256)} %bitcast.252, f32[256]{0:T(256)} %bitcast.253, ...), kind=kLoop, calls=%fused_computation.297 | loop fusion | flops 38534144 | bytes 26792960 | tf_op jit(solution)/shard_map/reduce_sum | solution.py:64
  131.8 0.6 copy.150
  132.4 0.4 multiply_reduce_fusion.2
  132.8 0.1 copy.151
  132.8 0.1 div.15
  132.9 0.1 copy.152
  133.0 0.1 rsqrt.12
  133.1 0.3 multiply_convert_fusion.1
  133.5 1.7 multiply_convert_fusion
  135.2 1.3 fusion.7
  136.5 1.8 fusion.107
  138.3 3.4 %fusion.6 = bf16[1024,1024]{1,0:T(8,128)(2,1)S(1)} fusion(f32[1024,1024]{1,0:T(8,128)S(1)} %get-tuple-element.225, bf16[1024,256]{1,0:T(8,128)(2,1)S(1)} %copy-done.8, bf16[1024,256]{1,0:T(8,128)(2,1)S(1)} %bitcast.291, f32[256]{0:T(256)S(1)} %copy-done.10), kind=kOutput, calls=%fused_computation.9 | convolution fusion | flops 558628864 | bytes 7341056 | tf_op jit(solution)/shard_map/dot_general | solution.py:46
  141.6 0.7 fusion.115
  142.4 1.5 multiply_reduce_fusion
  143.9 1.0 subtract_multiply_fusion
  144.9 2.4 fusion.45
  147.3 3.2 %fusion.86 = (f32[256]{0:T(256)S(1)}, f32[256]{0:T(256)S(1)}, f32[256]{0:T(256)S(1)}, f32[256]{0:T(256)S(1)}, f32[256]{0:T(256)S(1)}, /*index=5*/f32[256]{0:T(25...) fusion(bf16[1,38,38,256]{3,1,2,0:T(8,128)(2,1)S(1)} %bitcast.17, ...), kind=kLoop, calls=%fused_computation.190 | loop fusion | flops 14151168 | bytes 10504192 | tf_op jit(solution)/shard_map/reduce_sum | solution.py:92
  150.5 3.8 %fusion.104 = (f32[256]{0:T(256)S(1)}, f32[256]{0:T(256)S(1)}, f32[256]{0:T(256)S(1)}, f32[256]{0:T(256)S(1)}, f32[256]{0:T(256)S(1)}, /*index=5*/f32[256]{0:T(2...) fusion(bf16[1,38,38,256]{3,1,2,0:T(8,128)(2,1)S(1)} %bitcast.17, ...), kind=kLoop, calls=%fused_computation.208 | loop fusion | flops 14151168 | bytes 10504192 | tf_op jit(solution)/shard_map/reduce_sum | solution.py:92
  154.3 2.2 stack.219
  156.6 117.3 %all-reduce.3 = (f32[49,256]{1,0:T(8,128)}, f32[256]{0:T(256)}, f32[256]{0:T(256)}, bf16[256,1024]{1,0:T(8,128)(2,1)}, bf16[1024,256]{1,0:T(8,128)(2,1)}) all-reduce(f32[49,256]{1,0:T(8,128)S(1)} %stack.219, f32[256]{0:T(256)} %get-tuple-element.101, f32[256]{0:T(256)} %fusion.7, ...), channel_id=1, replica_groups=mesh['dp'=32,'space'=16] {'dp','space'}, use_global_device_ids=true, to_apply=%region_54.55 | all-reduce | flops 537344 | bytes 3250176 | tf_op jit(solution)/shard_map/psum | solution.py:114
  (39 shorter events, 0.3 us)
Async XLA Ops:
  7.2 126.3 %copy-start = (bf16[256,1024]{1,0:T(8,128)(2,1)S(1)}, bf16[256,1024]{1,0:T(8,128)(2,1)}, u32[]{:S(2)}) copy-start(bf16[256,1024]{1,0:T(8,128)(2,1)} %param.29) | copy-start | bytes 1572868
  7.2 4.2 %copy-start.7 = (s32[4]{0:T(128)S(1)}, s32[4]{0:T(128)}, u32[]{:S(2)}) copy-start(s32[4]{0:T(128)} %constant.206.clone.1) | copy-start | bytes 52
  7.2 3.1 %copy-start.4 = (s32[16,8]{0,1:T(8,128)S(1)}, s32[16,8]{0,1:T(8,128)}, u32[]{:S(2)}) copy-start(s32[16,8]{0,1:T(8,128)} %param.32) | copy-start | bytes 1540
  7.2 3.1 %copy-start.5 = (s32[16,8]{0,1:T(8,128)S(1)}, s32[16,8]{0,1:T(8,128)}, u32[]{:S(2)}) copy-start(s32[16,8]{0,1:T(8,128)} %param.33) | copy-start | bytes 1540
  7.2 4.9 %copy-start.3 = (bf16[49,256]{1,0:T(8,128)(2,1)S(1)}, bf16[49,256]{1,0:T(8,128)(2,1)}, u32[]{:S(2)}) copy-start(bf16[49,256]{1,0:T(8,128)(2,1)} %param.27) | copy-start | bytes 75268
  7.2 88.2 %all-gather.3.cloned.1.call-start = ((), (), s32[]{:S(2)}) async-start(), calls=%async_computation | async-start | bytes 3342336 | tf_op jit(solution)/shard_map/all_gather | solution.py:103
  103.1 13.6 %copy-start.2 = (bf16[1,1,3,32,256]{4,3,2,1,0:T(8,128)(2,1)S(1)}, bf16[1,1,3,32,256]{4,3,2,1,0:T(8,128)(2,1)}, u32[]{:S(2)}) copy-start(bf16[1,1,3,32,256]{4,3,2,1,0:T(8,128)(2,1)} %slice.678) | copy-start | bytes 147460
  122.3 10.8 %copy-start.6 = (f32[256]{0:T(256)S(1)}, f32[256]{0:T(256)}, u32[]{:S(2)}) copy-start(f32[256]{0:T(256)} %param.28) | copy-start | bytes 3076
  133.5 1.7 copy-start.8
  133.5 1.7 copy-start.9
  135.2 1.3 copy-start.10
  150.5 6.1 %copy-start.1 = (f32[1024,256]{1,0:T(8,128)S(1)}, f32[1024,256]{1,0:T(8,128)}, u32[]{:S(2)}) copy-start(f32[1024,256]{1,0:T(8,128)} %fusion.107) | copy-start | bytes 3145732
Sparse Core Ops, SparseCore 0:
  10.7 84.6 all-gather.2
where the time goes:
time: 281 us
  blocking collectives  117 us (42%)
  waiting for transfers between devices  81.3 us (29%)
  other arithmetic  32.3 us (11%)
  local copies, waits for them, and re-layouts  24.8 us (9%)
  between operations  14.6 us (5%)
  matrix products  10.3 us (4%)
    psum x1, blocking collectives, on_device(): lax.psum((kernel_grad, gain_grad, scale_grad, in_grad, out_grad), ('dp',...  117 us
    all_gather x1, waiting for transfers between devices, on_device(): lax.all_gather(as_sent(strips), 'space', axis=0, tiled=True)  81.3 us
    reduce_sum x3, other arithmetic, block_grads(): kernel_rows.append(jnp.sum(depth_grad * window, axis=(0, 1, 2)))  9.46 us
    reduce_sum x1, other arithmetic, block_grads(): centered = flat - jnp.mean(flat, axis=-1, keepdims=True)  9.42 us
    another operation x6, other arithmetic  8.67 us
    scatter x8, local copies, waits for them, and re-layouts, build_frame(): turned.at[0:3, 3:-3].set(pieces[turn]).at[0:3, 0:3].set(blocks[turn])  7.07 us
  transfers between devices with their start and end apart: 1, of which 1 were waited for; matrix products, arithmetic and copies ran while one was open for 1% of the time, Pallas kernels for 0%

commit v1 on v0

v1 whole, which is shorter than its diff:
```python
import jax
import jax.numpy as jnp
from jax import lax
from jax.experimental import pallas as pl
from jax.experimental.pallas import tpu as pltpu
from jax.sharding import PartitionSpec as P

EPSILON = 1e-06
MESH = pl.DeviceIdType.MESH
F32 = jnp.float32
BF16 = jnp.bfloat16

CORES, NX, NY_LO, NY_HI, NZ = 2, 4, 4, 2, 8
NY = NY_LO * NY_HI

S = 32
C = 256
HID = 1024
PIX = S * S
PITCH = 40
ROWS = 38


class Place:
    def __init__(self):
        dp = lax.axis_index("dp")
        space = lax.axis_index("space")
        self.core = lax.rem(dp, CORES)
        self.y_hi = lax.rem(dp // CORES, NY_HI)
        self.z = dp // (CORES * NY_HI)
        self.x = lax.rem(space, NX)
        self.y_lo = space // NX
        self.y = self.y_hi * NY_LO + self.y_lo
        self.dp = dp
        self.space = space

    def at(self, core=None, x=None, y=None, z=None):
        core = self.core if core is None else core
        x = self.x if x is None else x
        y = self.y if y is None else y
        z = self.z if z is None else z
        dp = (z * NY_HI + y // NY_LO) * CORES + core
        return {"dp": dp, "space": lax.rem(y, NY_LO) * NX + x}


def greet(devices):
    barrier = pltpu.get_barrier_semaphore()
    for device in devices:
        pl.semaphore_signal(barrier, inc=1, device_id=device, device_id_type=MESH)
    pl.semaphore_wait(barrier, len(devices))


class Copies:
    def __init__(self, send_sems, recv_sems):
        self.send_sems = send_sems
        self.recv_sems = recv_sems
        self.used = 0
        self.started = []

    def send(self, src, dst, device):
        copy = pltpu.make_async_remote_copy(
            src_ref=src,
            dst_ref=dst,
            send_sem=self.send_sems.at[self.used],
            recv_sem=self.recv_sems.at[self.used],
            device_id=device,
            device_id_type=MESH,
        )
        copy.start()
        self.used += 1
        self.started.append(copy)
        return copy

    def finish(self):
        for copy in self.started:
            copy.wait_send()


def rim_kernel(ids, codes, x_ref, sides, corners, xf, gath, out_s, out_c, in_s, in_c, cf, ss, rs):
    me = Place()
    y_lo, x = me.y_lo, me.x
    base = me.y_hi * NY_LO
    turn = reversal()
    xf[...] = x_ref[...].astype(F32)
    for r in range(3):
        gath[y_lo, 0, r] = x_ref[r]
        gath[y_lo, 2, r] = flip(turn, x_ref[S - 1 - r])
        gath[y_lo, 1, r] = xf[:, S - 1 - r, :].astype(BF16)
        gath[y_lo, 3, r] = flip(turn, xf[:, r, :].astype(BF16))
    along_y = [me.at(y=base + lax.rem(y_lo + k, NY_LO)) for k in range(1, NY_LO)]
    along_x = [me.at(x=lax.rem(x + k, NX)) for k in range(1, NX)]
    greet(along_y + along_x)
    net = Copies(ss, rs)
    first = [net.send(gath.at[y_lo], gath.at[y_lo], device) for device in along_y]
    for copy in first:
        copy.wait_recv()
    second = []
    for k in (2, 1, 3, 0):
        target = y_lo * NX + lax.rem(x + k, NX)
        for s in range(8):
            n = jnp.maximum(ids[target, s], 0)
            row = n // NX
            e = codes[target, s]
            if s < 4:
                piece = gath[row, e]
                if k:
                    out_s[k - 1, s] = piece
                else:
                    in_s[x, s] = piece
            else:
                piece = gath[row, e, :, 0:16, :].astype(F32)
                for r in range(3):
                    cf[pl.ds(16 * (s - 4) + 4 * r, 4), :] = piece[r, 0:4]
        if k:
            out_c[k - 1] = cf[...].astype(BF16)
            second.append(net.send(out_s.at[k - 1], in_s.at[x], along_x[k - 1]))
            second.append(net.send(out_c.at[k - 1], in_c.at[x], along_x[k - 1]))
        else:
            in_c[x] = cf[...].astype(BF16)
    for copy in second:
        copy.wait_recv()
    for s in range(8):
        n = ids[me.space, s]
        col = lax.rem(jnp.maximum(n, 0), NX)
        if s < 4:
            sides[s] = in_s[col, s]
        else:
            piece = in_c[col, pl.ds(16 * (s - 4), 16)]
            corners[s - 4] = jnp.where(n >= 0, piece, jnp.zeros_like(piece))
    net.finish()


def reversal():
    row = lax.broadcasted_iota(jnp.int32, (S, S), 0)
    col = lax.broadcasted_iota(jnp.int32, (S, S), 1)
    return jnp.where(row + col == S - 1, 1.0, 0.0).astype(BF16)


def flip(turn, rows):
    return jnp.dot(turn, rows, preferred_element_type=F32).astype(rows.dtype)


def exchange_rims(tile, neighbours, codes):
    copies = 3 + 6
    return pl.pallas_call(
        rim_kernel,
        out_shape=(
            jax.ShapeDtypeStruct((4, 3, S, C), BF16),
            jax.ShapeDtypeStruct((4, 16, C), BF16),
        ),
        in_specs=[
            pl.BlockSpec(memory_space=pltpu.SMEM),
            pl.BlockSpec(memory_space=pltpu.SMEM),
            pl.BlockSpec(memory_space=pltpu.VMEM),
        ],
        out_specs=(pl.BlockSpec(memory_space=pltpu.VMEM), pl.BlockSpec(memory_space=pltpu.VMEM)),
        scratch_shapes=[
            pltpu.VMEM((S, S, C), F32),
            pltpu.VMEM((NY_LO, 4, 3, S, C), BF16),
            pltpu.VMEM((NX - 1, 4, 3, S, C), BF16),
            pltpu.VMEM((NX - 1, 64, C), BF16),
            pltpu.VMEM((NX, 4, 3, S, C), BF16),
            pltpu.VMEM((NX, 64, C), BF16),
            pltpu.VMEM((64, C), F32),
            pltpu.SemaphoreType.DMA((copies,)),
            pltpu.SemaphoreType.DMA((copies,)),
        ],
        compiler_params=pltpu.CompilerParams(
            collective_id=0, has_side_effects=True, vmem_limit_bytes=32 * 2**20
        ),
    )(neighbours, codes, tile)


def build_frame(x_ref, sides, corners, fr, cf):
    turn = reversal()

    def interior(i, carry):
        fr[3 + i, 3 : 3 + S, :] = x_ref[i].astype(F32)
        return carry

    lax.fori_loop(0, S, interior, 0)
    for r in range(3):
        fr[r, 3 : 3 + S, :] = flip(turn, sides[0, 2 - r]).astype(F32)
        fr[3 : 3 + S, 35 + r, :] = flip(turn, sides[1, r]).astype(F32)
        fr[35 + r, 3 : 3 + S, :] = sides[2, r].astype(F32)
        fr[3 : 3 + S, r, :] = sides[3, 2 - r].astype(F32)
    cf[...] = corners[...].astype(F32)
    for i in range(3):
        for j in range(3):
            fr[i, j, :] = cf[0, 4 * (2 - i) + 2 - j, :]
            fr[i, 35 + j, :] = cf[1, 4 * j + 2 - i, :]
            fr[35 + i, 35 + j, :] = cf[2, 4 * i + j, :]
            fr[35 + i, j, :] = cf[3, 4 * (2 - j) + i, :]


def shift_frame(fr, fb):
    def one_row(i, carry):
        for b in range(7):
            fb[b, i] = fr[i, b : b + S, :]
        return carry

    lax.fori_loop(0, ROWS, one_row, 0)


def lanes(g):
    return (
        pl.ds(pl.multiple_of((g // 2) * 8, 8), 8),
        pl.ds(pl.multiple_of(lax.rem(g, 2) * 128, 128), 128),
    )


def depthwise(fb, taps, dw):
    def step(g, carry):
        cols, chans = lanes(g)
        acc = [None] * S
        for b in range(7):
            k = [jnp.broadcast_to(taps[pl.ds(7 * a + b, 1), chans], (8, 128)) for a in range(7)]
            for i in range(ROWS):
                f = fb[b, i, cols, chans]
                for a in range(7):
                    at = i - a
                    if 0 <= at < S:
                        term = f * k[a]
                        acc[at] = term if acc[at] is None else acc[at] + term
        for i in range(S):
            dw[i, cols, chans] = acc[i]
        return carry

    lax.fori_loop(0, 8, step, 0)


def correlate(fb, dg, kg):
    def step(g, carry):
        cols, chans = lanes(g)
        d = [dg[i, cols, chans] for i in range(S)]
        for b in range(7):
            acc = [None] * 7
            for i in range(ROWS):
                f = fb[b, i, cols, chans]
                for a in range(7):
                    at = i - a
                    if 0 <= at < S:
                        term = f * d[at]
                        acc[a] = term if acc[a] is None else acc[a] + term
            for a in range(7):
                kg[7 * a + b, :, chans] += acc[a]
        return carry

    kg[...] = jnp.zeros_like(kg)
    lax.fori_loop(0, 8, step, 0)


def gelu_and_slope(v):
    root = 0.7978845608028654
    square = v * v
    inner = v * (root + (root * 0.044715) * square)
    t = jnp.tanh(inner)
    half = 0.5 * (1.0 + t)
    slope = half + (0.5 * v) * (1.0 - t * t) * (root + (3.0 * root * 0.044715) * square)
    return v * half, slope


def nt(left, right):
    return lax.dot_general(left, right, (((1,), (1,)), ((), ())), preferred_element_type=F32)


def block_kernel(
    x_ref, cot, taps_in, gain, w_in, w_in_t, w_out, layer, sides, corners,
    big, small,
    fr, cf, fb, taps, dw, inv, scaled, scaled_t, branch, pre, hg, hid, pg, sg_t, kg,
):
    build_frame(x_ref, sides, corners, fr, cf)
    shift_frame(fr, fb)
    taps[...] = taps_in[...].astype(F32)
    depthwise(fb, taps, dw)

    def norm(q, carry):
        rows = pl.ds(q * 4, 4)
        flat = pl.ds(pl.multiple_of(q * 128, 128), 128)
        v = dw[rows].reshape(128, C)
        mean = jnp.mean(v, axis=-1, keepdims=True)
        v = v - mean
        inverse = lax.rsqrt(jnp.mean(v * v, axis=-1, keepdims=True) + EPSILON)
        normed = v * inverse
        inv[flat] = jnp.broadcast_to(inverse, (128, 128))
        dw[rows] = normed.reshape(4, S, C)
        scaled[flat] = (normed * gain[...]).astype(BF16)
        branch[flat] = (cot[flat].astype(F32) * layer[...]).astype(BF16)
        return carry

    lax.fori_loop(0, 8, norm, 0)
    scaled_t[...] = scaled[...].T

    scale_grad = jnp.zeros((1, C), F32)
    for h in range(HID // 256):
        part = slice(256 * h, 256 * h + 256)
        pre[...] = jnp.dot(w_in_t[part], scaled_t[...], preferred_element_type=F32)
        hg[...] = nt(w_out[part], branch[...])

        def act(q, carry):
            rows = pl.ds(pl.multiple_of(q * 16, 16), 16)
            out = pl.ds(pl.multiple_of(256 * h + q * 16, 16), 16)
            value, slope = gelu_and_slope(pre[rows])
            hid[rows] = value.astype(BF16)
            pg[out] = (hg[rows] * slope).astype(BF16)
            return carry

        lax.fori_loop(0, 16, act, 0)
        g = jnp.dot(hid[...], cot[...], preferred_element_type=F32)
        big[part] = (g * layer[...]).astype(BF16)
        scale_grad += jnp.sum(g * w_out[part].astype(F32), axis=0, keepdims=True)
        big[slice(HID + 256 * h, HID + 256 * h + 256)] = nt(scaled_t[...], pg[part]).astype(BF16)
    sg_t[...] = jnp.dot(w_in[...], pg[...], preferred_element_type=F32)

    gain_grad = jnp.zeros((1, C), F32)
    for q in range(8):
        rows = slice(4 * q, 4 * q + 4)
        flat = slice(128 * q, 128 * q + 128)
        normed = dw[rows].reshape(128, C)
        sg = sg_t[:, flat].T
        gain_grad += jnp.sum(sg * normed, axis=0, keepdims=True)
        g = sg * gain[...]
        mean = jnp.mean(g, axis=-1, keepdims=True)
        along = jnp.mean(g * normed, axis=-1, keepdims=True)
        inverse = inv[flat]
        grad = (g - mean - normed * along) * jnp.concatenate([inverse, inverse], axis=1)
        dw[rows] = grad.reshape(4, S, C)
    correlate(fb, dw, kg)
    small[0:49] = jnp.sum(kg[...], axis=1)
    small[49:50] = gain_grad
    small[50:51] = scale_grad
    small[51:64] = jnp.zeros((13, C), F32)


def own_grads(tile, cot, kernel, ln_gain, w_in, w_out, layer_scale, sides, corners):
    vmem = pl.BlockSpec(memory_space=pltpu.VMEM)
    return pl.pallas_call(
        block_kernel,
        out_shape=(
            jax.ShapeDtypeStruct((2 * HID, C), BF16),
            jax.ShapeDtypeStruct((64, C), F32),
        ),
        in_specs=[vmem] * 10,
        out_specs=(vmem, vmem),
        scratch_shapes=[
            pltpu.VMEM((ROWS, PITCH, C), F32),
            pltpu.VMEM((4, 16, C), F32),
            pltpu.VMEM((7, ROWS, S, C), F32),
            pltpu.VMEM((49, C), F32),
            pltpu.VMEM((S, S, C), F32),
            pltpu.VMEM((PIX, 128), F32),
            pltpu.VMEM((PIX, C), BF16),
            pltpu.VMEM((C, PIX), BF16),
            pltpu.VMEM((PIX, C), BF16),
            pltpu.VMEM((256, PIX), F32),
            pltpu.VMEM((256, PIX), F32),
            pltpu.VMEM((256, PIX), BF16),
            pltpu.VMEM((HID, PIX), BF16),
            pltpu.VMEM((C, PIX), F32),
            pltpu.VMEM((49, 8, C), F32),
        ],
        compiler_params=pltpu.CompilerParams(vmem_limit_bytes=48 * 2**20),
    )(
        tile, cot, kernel, ln_gain.reshape(1, C), w_in, w_in.T, w_out,
        layer_scale.reshape(1, C), sides, corners,
    )


def sum_kernel(
    big, small, kg_out, gain_out, scale_out, in_out, out_out,
    r0, s1, r1, s2, r2, s3, r3, fin, q0, t1, q1, t2, q2, t3, q3, sfin, ss, rs,
):
    me = Place()
    core, x, y, z = me.core, me.x, me.y, me.z
    other = 1 - core
    mate = me.at(core=other)
    along_x = [me.at(x=lax.rem(x + k, NX)) for k in range(1, NX)]
    along_y = [me.at(y=lax.rem(y + k, NY)) for k in range(1, NY)]
    along_z = [me.at(z=lax.rem(z + k, NZ)) for k in range(1, NZ)]
    greet([mate] + along_x + along_y + along_z)
    net = Copies(ss, rs)
    far_first = (4, 3, 5, 2, 6, 1, 7)

    halves = []
    small_half = net.send(
        small.at[pl.ds(pl.multiple_of(other * 32, 32), 32)], q0, mate
    )
    order = (2, 1, 3, 0)
    for k in order:
        at = lax.rem(x + k, NX)
        halves.append(
            net.send(
                big.at[pl.ds(pl.multiple_of(other * HID + at * 256, 256), 256)], r0.at[at], mate
            )
        )
    small_half.wait_recv()
    t1[...] = (small[pl.ds(pl.multiple_of(core * 32, 32), 32)] + q0[...]).reshape(NX, 8, C)
    small_x = [
        net.send(t1.at[lax.rem(x + k, NX)], q1.at[k - 1], along_x[k - 1]) for k in range(1, NX)
    ]
    big_x = []
    for k, copy in zip(order, halves):
        at = lax.rem(x + k, NX)
        copy.wait_recv()
        own = big[pl.ds(pl.multiple_of(core * HID + at * 256, 256), 256)]
        s1[at] = (own.astype(F32) + r0[at].astype(F32)).astype(BF16)
        if k:
            big_x.append(net.send(s1.at[at], r1.at[k - 1], along_x[k - 1]))

    for copy in small_x:
        copy.wait_recv()
    t2[...] = t1[x] + q1[0] + q1[1] + q1[2]
    q2[y] = t2[...]
    small_y = [net.send(t2, q2.at[y], along_y[k - 1]) for k in far_first]
    for copy in big_x:
        copy.wait_recv()
    total = s1[x].astype(F32)
    for k in range(NX - 1):
        total += r1[k].astype(F32)
    s2[...] = total.astype(BF16).reshape(NY, 32, C)
    big_y = [
        net.send(s2.at[lax.rem(y + k, NY)], r2.at[k - 1], along_y[k - 1]) for k in far_first
    ]
    for copy in small_y:
        copy.wait_recv()
    t3[...] = jnp.sum(q2[...], axis=0)
    q3[z] = t3[...]
    small_z = [net.send(t3, q3.at[z], along_z[k - 1]) for k in far_first]
    for copy in big_y:
        copy.wait_recv()
    total = s2[y].astype(F32)
    for k in range(NY - 1):
        total += r2[k].astype(F32)
    s3[...] = total.astype(BF16)
    r3[z] = s3[...]
    big_z = [net.send(s3, r3.at[z], along_z[k - 1]) for k in far_first]
    for copy in small_z:
        copy.wait_recv()
    sfin[core, x] = jnp.sum(q3[...], axis=0)
    small_back = [net.send(sfin.at[core, x], sfin.at[core, x], device) for device in along_x]
    for copy in big_z:
        copy.wait_recv()
    total = r3[0].astype(F32)
    for k in range(1, NZ):
        total += r3[k].astype(F32)
    fin[core, x, y] = total.astype(BF16)

    back_y = [
        net.send(fin.at[core, x, y], fin.at[core, x, y], along_y[k - 1]) for k in far_first
    ]
    for copy in small_back:
        copy.wait_recv()
    small_mate = net.send(sfin.at[core], sfin.at[core], mate)
    for copy in back_y:
        copy.wait_recv()
    back_x = [
        net.send(fin.at[core, x], fin.at[core, x], along_x[k - 1]) for k in (2, 1, 3)
    ]
    back_mate = [net.send(fin.at[core, x], fin.at[core, x], mate)]
    for k, copy in zip((2, 1, 3), back_x):
        copy.wait_recv()
        at = lax.rem(x + NX - k, NX)
        back_mate.append(net.send(fin.at[core, at], fin.at[core, at], mate))
    small_mate.wait_recv()
    rows = sfin[...].reshape(64, C)
    kg_out[...] = rows[0:49]
    gain_out[...] = rows[49:50]
    scale_out[...] = rows[50:51]
    for copy in back_mate:
        copy.wait_recv()
    out_out[...] = fin[0].reshape(HID, C)
    for q in range(NX):
        in_out[:, 256 * q : 256 * q + 256] = fin[1, q].reshape(256, C)
    net.finish()


def sum_grads(big, small):
    vmem = pl.BlockSpec(memory_space=pltpu.VMEM)
    copies = 1 + 4 + 3 + 3 + 7 * 5 + 3 + 1 + 3 + 4
    return pl.pallas_call(
        sum_kernel,
        out_shape=(
            jax.ShapeDtypeStruct((49, C), F32),
            jax.ShapeDtypeStruct((1, C), F32),
            jax.ShapeDtypeStruct((1, C), F32),
            jax.ShapeDtypeStruct((C, HID), BF16),
            jax.ShapeDtypeStruct((HID, C), BF16),
        ),
        in_specs=[vmem, vmem],
        out_specs=(vmem,) * 5,
        scratch_shapes=[
            pltpu.VMEM((NX, 256, C), BF16),
            pltpu.VMEM((NX, 256, C), BF16),
            pltpu.VMEM((NX - 1, 256, C), BF16),
            pltpu.VMEM((NY, 32, C), BF16),
            pltpu.VMEM((NY - 1, 32, C), BF16),
            pltpu.VMEM((32, C), BF16),
            pltpu.VMEM((NZ, 32, C), BF16),
            pltpu.VMEM((2, NX, NY, 32, C), BF16),
            pltpu.VMEM((32, C), F32),
            pltpu.VMEM((NX, 8, C), F32),
            pltpu.VMEM((NX - 1, 8, C), F32),
            pltpu.VMEM((8, C), F32),
            pltpu.VMEM((NY, 8, C), F32),
            pltpu.VMEM((8, C), F32),
            pltpu.VMEM((NZ, 8, C), F32),
            pltpu.VMEM((2, NX, 8, C), F32),
            pltpu.SemaphoreType.DMA((copies,)),
            pltpu.SemaphoreType.DMA((copies,)),
        ],
        compiler_params=pltpu.CompilerParams(
            collective_id=1, has_side_effects=True, vmem_limit_bytes=32 * 2**20
        ),
    )(big, small)


def on_device(state, cotangent, kernel, ln_gain, w_in, w_out, layer_scale, neighbours, codes):
    tile = state.reshape(S, S, C)
    cot = cotangent.reshape(PIX, C)
    sides, corners = exchange_rims(tile, neighbours, codes)
    big, small = own_grads(
        tile, cot, kernel, ln_gain, w_in, w_out, layer_scale, sides, corners
    )
    kernel_grad, gain_grad, scale_grad, in_grad, out_grad = sum_grads(big, small)
    return (kernel_grad, gain_grad.reshape(C), scale_grad.reshape(C), in_grad, out_grad)


def solution(mesh):
    placed = (P("dp", "space", None, None, None),) * 2 + (P(),) * 7
    return jax.shard_map(
        on_device, mesh=mesh, in_specs=placed, out_specs=(P(),) * 5, check_vma=False
    )
```

time: 281 us -> 111 us (0.40)
  blocking collectives: 117 us -> 0 us
  Pallas kernels: 0 us -> 102 us
  waiting for transfers between devices: 81.3 us -> 0 us
  other arithmetic: 32.3 us -> 0 us
  local copies, waits for them, and re-layouts: 24.8 us -> 8.78 us
  between operations: 14.6 us -> 0.72 us
  matrix products: 10.3 us -> 0 us
    psum x1 -> x0, blocking collectives: 117 us -> none  [on_device(): lax.psum((kernel_grad, gain_grad, scale_grad, in_grad, out_grad), ('dp',...]
    pallas_call x0 -> x3, Pallas kernels: none -> 102 us  [the longest x1 51.1 us: sum_grads(): pl.pallas_call(sum_kernel, out_shape=(jax.ShapeDtypeStruct((49, C), F32),...]
    all_gather x1 -> x0, waiting for transfers between devices: 81.3 us -> none  [on_device(): lax.all_gather(as_sent(strips), 'space', axis=0, tiled=True)]
    reduce_sum x5 -> x0, other arithmetic: 19.3 us -> none  [the longest x3 9.46 us: block_grads(): kernel_rows.append(jnp.sum(depth_grad * window, axis=(0, 1, 2)))]
    dot_general x6 -> x0, matrix products: 10.3 us -> none  [the longest x2 4.86 us: inner_cols(): lax.dot_general(left, right, (((1,), (1,)), ((), ())), preferred_element_...]
    another operation x7 -> x0, other arithmetic: 9.38 us -> none
    rev x6 -> x0, local copies, waits for them, and re-layouts: 7.76 us -> none  [the longest x3 3.86 us: build_frame(): turned = jnp.rot90(frame, turn, axes=(0, 1))]
    unnamed x25 -> x28, local copies, waits for them, and re-layouts: 1.53 us -> 8.78 us
  transfers between devices with their start and end apart: 1 -> 0, of which waited for: 1 -> 0; matrix products, arithmetic and copies ran while one was open for 1% -> 0% of each run, Pallas kernels for 0% -> 0%
where the time goes in v1:
time: 111 us
  Pallas kernels  102 us (92%)
  local copies, waits for them, and re-layouts  8.78 us (8%)
    pallas_call x1, Pallas kernels, sum_grads(): pl.pallas_call(sum_kernel, out_shape=(jax.ShapeDtypeStruct((49, C), F32),...  51.1 us
    pallas_call x1, Pallas kernels, exchange_rims(): pl.pallas_call(rim_kernel, out_shape=(jax.ShapeDtypeStruct((4, 3, S, C),...  32.6 us
    pallas_call x1, Pallas kernels, own_grads(): pl.pallas_call(block_kernel, out_shape=(jax.ShapeDtypeStruct((2 * HID, C)...  17.7 us
    unnamed x28, local copies, waits for them, and re-layouts  8.78 us

profile of v1, /device:TPU:1, one launch (start us, length us, event | category | flops | bytes accessed | tf_op | source)
XLA Modules:
  0.0 111.0 jit_solution(10446747182108732280)
XLA Ops:
  0.6 0.0 copy-start.8
  0.6 0.7 copy-done.8
  1.3 0.0 copy-start.9
  1.3 0.1 copy.15.ids
  1.4 0.6 copy-done.9
  2.0 0.1 copy.16.codes
  2.1 0.0 copy-start
  2.1 1.0 copy-done
  3.1 0.0 copy-start.2
  3.1 0.0 copy-start.7
  3.1 32.6 %shard_map.128 = (bf16[4,3,32,256]{3,2,1,0:T(8,128)(2,1)S(1)}, bf16[4,16,256]{2,1,0:T(8,128)(2,1)S(1)}) custom-call(s32[16,8]{1,0:T(8,128)S(1)} %copy.15.ids, s32[16,8]{1,0:T(8,128)S(1)} %copy.16.codes, bf16[32,32,256]{2,1,0:T(8,128)(2,1)S(1)} %bitcast.7), custom_call_target="tpu_custom_call" | custom-call | tf_op jit(solution)/shard_map/pallas_call | solution.py:145
  35.8 0.0 copy-done.2
  35.8 0.0 copy-start.1
  35.8 0.0 copy-start.3
  35.8 0.2 copy.14
  36.0 0.0 copy-start.6
  36.0 0.0 copy-done.7
  36.0 0.8 copy-done.1
  36.8 0.2 copy-done.3
  37.0 0.0 copy-done.6
  37.0 0.0 copy-start.4
  37.0 1.0 copy-done.4
  38.0 0.0 copy-start.5
  38.0 0.7 copy-done.5
  38.8 17.7 %shard_map.129 = (bf16[2048,256]{1,0:T(8,128)(2,1)S(1)}, f32[64,256]{1,0:T(8,128)S(1)}) custom-call(bf16[32,32,256]{2,1,0:T(8,128)(2,1)S(1)} %bitcast.8, bf16[1024,256]{1,0:T(8,128)(2,1)S(1)} %bitcast.10, bf16[49,256]{1,0:T(8,128)(2,1)S(1)} %copy-done.5, f32[1,256]{1,0:T(1,128)S(1)} %bitcast.11, bf16[256,1024]{1,0:T(8,128)(2,1)S(1)} %copy-done.2, ...), custom_call_target="tpu_custom_call" | custom-call | tf_op jit(solution)/shard_map/pallas_call | solution.py:337
  56.5 51.1 %shard_map.130 = (f32[49,256]{1,0:T(8,128)S(1)}, f32[1,256]{1,0:T(1,128)S(1)}, f32[1,256]{1,0:T(1,128)S(1)}, bf16[256,1024]{1,0:T(8,128)(2,1)S(1)}, bf16[1024,256]{1,0:T(8,128)(2,1)S(1)}) custom-call(bf16[2048,256]{1,0:T(8,128)(2,1)S(1)} %get-tuple-element.16.big, f32[64,256]{1,0:T(8,128)S(1)} %get-tuple-element.17.small), custom_call_target="tpu_custom_call" | custom-call | tf_op jit(solution)/shard_map/pallas_call | solution.py:480
  107.7 0.6 copy.22
  108.3 0.6 copy.23
  108.8 0.6 copy.24
  109.4 0.8 copy.25
  110.2 0.8 copy.26
Async XLA Ops:
  0.6 0.7 copy-start.8
  1.3 0.7 copy-start.9
  2.1 1.0 copy-start
  3.1 32.7 %copy-start.2 = (bf16[256,1024]{1,0:T(8,128)(2,1)S(1)}, bf16[256,1024]{1,0:T(8,128)(2,1)}, u32[]{:S(2)}) copy-start(bf16[256,1024]{1,0:T(8,128)(2,1)} %w_in.1) | copy-start | bytes 1572868
  3.1 32.9 %copy-start.7 = (f32[256]{0:T(256)S(1)}, f32[256]{0:T(256)}, u32[]{:S(2)}) copy-start(f32[256]{0:T(256)} %param.15) | copy-start | bytes 3076
  35.8 1.0 copy-start.1
  35.8 1.2 %copy-start.3 = (bf16[1,1,32,32,256]{4,3,2,1,0:T(8,128)(2,1)S(1)}, bf16[1,1,32,32,256]{4,3,2,1,0:T(8,128)(2,1)}, u32[]{:S(2)}) copy-start(bf16[1,1,32,32,256]{4,3,2,1,0:T(8,128)(2,1)} %param.10) | copy-start | bytes 1572868
  36.0 1.0 copy-start.6
  37.0 1.0 copy-start.4
  38.0 0.7 copy-start.5

commit v2 on v0

v2 whole, which is shorter than its diff:
```python
import jax
import jax.numpy as jnp
from jax import lax
from jax.experimental import pallas as pl
from jax.experimental.pallas import tpu as pltpu
from jax.sharding import PartitionSpec as P

EPSILON = 1e-06
MESH = pl.DeviceIdType.MESH
F32 = jnp.float32
BF16 = jnp.bfloat16

CORES, NX, NY_LO, NY_HI, NZ = 2, 4, 4, 2, 8
NY = NY_LO * NY_HI

S = 32
C = 256
HID = 1024
PIX = S * S
PITCH = 40
ROWS = 38


class Place:
    def __init__(self):
        dp = lax.axis_index("dp")
        space = lax.axis_index("space")
        self.core = lax.rem(dp, CORES)
        self.y_hi = lax.rem(dp // CORES, NY_HI)
        self.z = dp // (CORES * NY_HI)
        self.x = lax.rem(space, NX)
        self.y_lo = space // NX
        self.y = self.y_hi * NY_LO + self.y_lo
        self.dp = dp
        self.space = space

    def at(self, core=None, x=None, y=None, z=None):
        core = self.core if core is None else core
        x = self.x if x is None else x
        y = self.y if y is None else y
        z = self.z if z is None else z
        dp = (z * NY_HI + y // NY_LO) * CORES + core
        return {"dp": dp, "space": lax.rem(y, NY_LO) * NX + x}


def greet(devices):
    barrier = pltpu.get_barrier_semaphore()
    for device in devices:
        pl.semaphore_signal(barrier, inc=1, device_id=device, device_id_type=MESH)
    pl.semaphore_wait(barrier, len(devices))


class Copies:
    def __init__(self, send_sems, recv_sems):
        self.send_sems = send_sems
        self.recv_sems = recv_sems
        self.used = 0
        self.started = []

    def send(self, src, dst, device):
        copy = pltpu.make_async_remote_copy(
            src_ref=src,
            dst_ref=dst,
            send_sem=self.send_sems.at[self.used],
            recv_sem=self.recv_sems.at[self.used],
            device_id=device,
            device_id_type=MESH,
        )
        copy.start()
        self.used += 1
        self.started.append(copy)
        return copy

    def finish(self):
        for copy in self.started:
            copy.wait_send()


HALF = C // 2


def own_strips(x_ref, xf, gath_y, gath_x, me):
    turn = reversal()
    xf[...] = x_ref[...].astype(F32)

    def put(side, r, rows):
        gath_y[me.y_lo, side, r] = rows[:, :HALF]
        gath_x[me.x, side, r] = rows[:, HALF:]

    for r in range(3):
        put(0, r, x_ref[r])
        put(2, r, flip(turn, x_ref[S - 1 - r]))
        put(1, r, xf[:, S - 1 - r, :].astype(BF16))
        put(3, r, flip(turn, xf[:, r, :].astype(BF16)))


class Rims:
    def __init__(self, net, ids, codes, gath, out_s, out_c, in_s, in_c, cf, gather_at, choose_at, gather_to, choose_to, tile_at, split):
        self.net = net
        self.ids, self.codes = ids, codes
        self.gath, self.out_s, self.out_c, self.in_s, self.in_c, self.cf = gath, out_s, out_c, in_s, in_c, cf
        self.gather_at, self.choose_at = gather_at, choose_at
        self.gather_to, self.choose_to = gather_to, choose_to
        self.tile_at, self.split = tile_at, split

    def gather(self):
        at = self.gather_at
        self.first = [
            self.net.send(self.gath.at[at], self.gath.at[at], self.gather_to[k - 1])
            for k in (2, 1, 3)
        ]

    def choose(self):
        for copy in self.first:
            copy.wait_recv()
        self.second = []
        at = self.choose_at
        for k in (2, 1, 3, 0):
            target = self.tile_at(lax.rem(at + k, 4))
            for s in range(8):
                row, _ = self.split(jnp.maximum(self.ids[target, s], 0))
                e = self.codes[target, s]
                if s < 4:
                    piece = self.gath[row, e]
                    if k:
                        self.out_s[k - 1, s] = piece
                    else:
                        self.in_s[at, s] = piece
                else:
                    piece = self.gath[row, e, :, 0:16, :].astype(F32)
                    for r in range(3):
                        self.cf[pl.ds(16 * (s - 4) + 4 * r, 4), :] = piece[r, 0:4]
            packed = self.cf[...].astype(BF16)
            if k:
                self.out_c[k - 1] = packed
                to = self.choose_to[k - 1]
                self.second.append(self.net.send(self.out_s.at[k - 1], self.in_s.at[at], to))
                self.second.append(self.net.send(self.out_c.at[k - 1], self.in_c.at[at], to))
            else:
                self.in_c[at] = packed

    def take(self, sides, corners, chans, space):
        for copy in self.second:
            copy.wait_recv()
        for s in range(8):
            n = self.ids[space, s]
            _, col = self.split(jnp.maximum(n, 0))
            if s < 4:
                sides[s, :, :, chans] = self.in_s[col, s]
            else:
                piece = self.in_c[col, pl.ds(16 * (s - 4), 16)]
                corners[s - 4, :, chans] = jnp.where(n >= 0, piece, jnp.zeros_like(piece))


def both_rims(net, me, ids, codes, along_y, along_x, bufs_y, bufs_x):
    by_y = Rims(
        net, ids, codes, *bufs_y, me.y_lo, me.x, along_y, along_x,
        lambda x: me.y_lo * NX + x, lambda n: (n // NX, lax.rem(n, NX)),
    )
    by_x = Rims(
        net, ids, codes, *bufs_x, me.x, me.y_lo, along_x, along_y,
        lambda y: y * NX + me.x, lambda n: (lax.rem(n, NX), n // NX),
    )
    return by_y, by_x


def rim_partners(me):
    base = me.y_hi * NY_LO
    along_y = [me.at(y=base + lax.rem(me.y_lo + k, NY_LO)) for k in range(1, NY_LO)]
    along_x = [me.at(x=lax.rem(me.x + k, NX)) for k in range(1, NX)]
    return along_y, along_x


RIM_COPIES = 2 * 9


def rim_scratch():
    half = [
        pltpu.VMEM((4, 4, 3, S, HALF), BF16),
        pltpu.VMEM((3, 4, 3, S, HALF), BF16),
        pltpu.VMEM((3, 64, HALF), BF16),
        pltpu.VMEM((4, 4, 3, S, HALF), BF16),
        pltpu.VMEM((4, 64, HALF), BF16),
        pltpu.VMEM((64, HALF), F32),
    ]
    return half * 2


def reversal():
    row = lax.broadcasted_iota(jnp.int32, (S, S), 0)
    col = lax.broadcasted_iota(jnp.int32, (S, S), 1)
    return jnp.where(row + col == S - 1, 1.0, 0.0).astype(BF16)


def flip(turn, rows):
    return jnp.dot(turn, rows, preferred_element_type=F32).astype(rows.dtype)


INNER = S - 6
IN_PIX = INNER * S
IN_PAD = 896
EDGE = 3 * S
SIDE_AT = 2 * EDGE
OUT_PIX = SIDE_AT + INNER * 8
OUT_PAD = 512


def frame_inside(xf, fr):
    fr[...] = jnp.zeros_like(fr)

    def one_row(i, carry):
        fr[3 + i, 3 : 3 + S, :] = xf[i]
        return carry

    lax.fori_loop(0, S, one_row, 0)


def frame_rims(sides, corners, fr, cf):
    turn = reversal()
    for r in range(3):
        fr[r, 3 : 3 + S, :] = flip(turn, sides[0, 2 - r]).astype(F32)
        fr[3 : 3 + S, 35 + r, :] = flip(turn, sides[1, r]).astype(F32)
        fr[35 + r, 3 : 3 + S, :] = sides[2, r].astype(F32)
        fr[3 : 3 + S, r, :] = sides[3, 2 - r].astype(F32)
    cf[...] = corners[...].astype(F32)
    for i in range(3):
        for j in range(3):
            fr[i, j, :] = cf[0, 4 * (2 - i) + 2 - j, :]
            fr[i, 35 + j, :] = cf[1, 4 * j + 2 - i, :]
            fr[35 + i, 35 + j, :] = cf[2, 4 * i + j, :]
            fr[35 + i, j, :] = cf[3, 4 * (2 - j) + i, :]


def shift_rows(fr, fb, first, count):
    def one_row(i, carry):
        for b in range(7):
            fb[b, first + i] = fr[first + i, b : b + S, :]
        return carry

    lax.fori_loop(0, count, one_row, 0)


def shift_sides(fr, fs):
    fs[...] = jnp.zeros_like(fs)

    def one_row(i, carry):
        for b in range(7):
            fs[b, i, 0:3, :] = fr[3 + i, b : b + 3, :]
            fs[b, i, 3:6, :] = fr[3 + i, 29 + b : 32 + b, :]
        return carry

    lax.fori_loop(0, S, one_row, 0)


def lanes(g):
    return (
        pl.ds(pl.multiple_of((g // 2) * 8, 8), 8),
        pl.ds(pl.multiple_of(lax.rem(g, 2) * 128, 128), 128),
    )


def convolve(load, taps, chans, count, put):
    acc = [None] * count
    for b in range(7):
        k = [jnp.broadcast_to(taps[pl.ds(7 * a + b, 1), chans], (8, 128)) for a in range(7)]
        for i in range(count + 6):
            f = load(b, i)
            for a in range(7):
                at = i - a
                if 0 <= at < count:
                    term = f * k[a]
                    acc[at] = term if acc[at] is None else acc[at] + term
    for i in range(count):
        put(i, acc[i])


def correlate(load, d, kg, chans):
    count = len(d)
    for b in range(7):
        acc = [None] * 7
        for i in range(count + 6):
            f = load(b, i)
            for a in range(7):
                at = i - a
                if 0 <= at < count:
                    term = f * d[at]
                    acc[a] = term if acc[a] is None else acc[a] + term
        for a in range(7):
            kg[7 * a + b, :, chans] += acc[a]


def normalise(v):
    mean = jnp.mean(v, axis=-1, keepdims=True)
    v = v - mean
    inverse = lax.rsqrt(jnp.mean(v * v, axis=-1, keepdims=True) + EPSILON)
    return v * inverse, inverse


def norm_backward(sg, normed, inverse, gain):
    g = sg * gain
    mean = jnp.mean(g, axis=-1, keepdims=True)
    along = jnp.mean(g * normed, axis=-1, keepdims=True)
    return (g - mean - normed * along) * jnp.concatenate([inverse, inverse], axis=1)


def gelu_and_slope(v):
    root = 0.7978845608028654
    square = v * v
    inner = v * (root + (root * 0.044715) * square)
    t = jnp.tanh(inner)
    half = 0.5 * (1.0 + t)
    slope = half + (0.5 * v) * (1.0 - t * t) * (root + (3.0 * root * 0.044715) * square)
    return v * half, slope


def dot(left, right):
    return jnp.dot(left, right, preferred_element_type=F32)


class Inside:
    def __init__(self, w, fb, bufs):
        self.w, self.fb = w, fb
        (self.normed, self.inv, self.scaled, self.cot, self.branch, self.scaled_t, self.cot_t,
         self.pre, self.hg, self.hid, self.pg, self.sg) = bufs

    def depthwise(self):
        def step(g, carry):
            cols, chans = lanes(g)

            def put(i, value):
                self.normed[i, cols, chans] = value

            convolve(lambda b, i: self.fb[b, 3 + i, cols, chans], self.w.taps, chans, INNER, put)
            return carry

        lax.fori_loop(0, 8, step, 0)

    def norm(self):
        w = self.w
        col = lax.rem(lax.broadcasted_iota(jnp.int32, (64, C), 0), S)
        here = (col >= 3) & (col < S - 3)

        def step(q, carry):
            rows = pl.ds(q * 2, 2)
            flat = pl.ds(pl.multiple_of(q * 64, 64), 64)
            normed, inverse = normalise(self.normed[rows].reshape(64, C))
            self.inv[flat] = jnp.broadcast_to(inverse, (64, 128))
            self.normed[rows] = normed.reshape(2, S, C)
            self.scaled[flat] = (normed * w.gain[...]).astype(BF16)
            cot = w.cot[pl.ds(pl.multiple_of(3 * S + q * 64, 32), 64)].astype(F32)
            cot = jnp.where(here, cot, jnp.zeros_like(cot))
            self.cot[flat] = cot.astype(BF16)
            self.branch[flat] = (cot * w.layer[...]).astype(BF16)
            return carry

        lax.fori_loop(0, INNER // 2, step, 0)
        rest = slice(IN_PIX, IN_PAD)
        none = jnp.zeros((IN_PAD - IN_PIX, C), BF16)
        self.scaled[rest] = none
        self.cot[rest] = none
        self.hid[rest] = none
        for h in range(4):
            self.pg[rest, 256 * h : 256 * h + 256] = none
        self.scaled_t[...] = self.scaled[...].T
        self.cot_t[...] = self.cot[...].T

    def hidden(self, h, gacc, iacc):
        w = self.w
        part = slice(256 * h, 256 * h + 256)
        self.pre[...] = dot(self.scaled[0:IN_PIX], w.w_in[:, part])
        self.hg[...] = dot(self.branch[...], w.w_out_t[:, part])

        def act(q, carry):
            rows = pl.ds(pl.multiple_of(q * 32, 32), 32)
            value, slope = gelu_and_slope(self.pre[rows])
            self.hid[rows] = value.astype(BF16)
            self.pg[rows, part] = (self.hg[rows] * slope).astype(BF16)
            return carry

        lax.fori_loop(0, IN_PIX // 32, act, 0)
        gacc[:, part] = dot(self.cot_t[...], self.hid[...])
        iacc[:, part] = dot(self.scaled_t[...], self.pg[:, part])

    def backward(self, gain_acc):
        w = self.w
        self.sg[...] = dot(self.pg[0:IN_PIX], w.w_in_t[...])

        def step(q, total):
            rows = pl.ds(q * 2, 2)
            flat = pl.ds(pl.multiple_of(q * 64, 64), 64)
            normed = self.normed[rows].reshape(64, C)
            sg = self.sg[flat]
            grad = norm_backward(sg, normed, self.inv[flat], w.gain[...])
            self.normed[rows] = grad.reshape(2, S, C)
            return total + jnp.sum((sg * normed).reshape(8, 8, C), axis=0)

        gain_acc[...] = lax.fori_loop(0, INNER // 2, step, jnp.zeros((8, C), F32))

    def kernel_grad(self, kg):
        def step(g, carry):
            cols, chans = lanes(g)
            d = [self.normed[i, cols, chans] for i in range(INNER)]
            correlate(lambda b, i: self.fb[b, 3 + i, cols, chans], d, kg, chans)
            return carry

        lax.fori_loop(0, 8, step, 0)


class Border:
    def __init__(self, w, fb, fs, bufs):
        self.w, self.fb, self.fs = w, fb, fs
        (self.normed, self.inv, self.scaled, self.cot, self.branch, self.scaled_t, self.cot_t,
         self.pre, self.hg, self.hid, self.pg, self.sg, self.cf) = bufs

    def cotangent(self):
        w = self.w
        self.cf[...] = jnp.zeros_like(self.cf)
        self.cf[0:EDGE] = w.cot[0:EDGE].astype(F32)
        self.cf[EDGE : 2 * EDGE] = w.cot[PIX - EDGE : PIX].astype(F32)
        for i in range(INNER):
            row = w.cot[(3 + i) * S : (4 + i) * S].astype(F32)
            at = SIDE_AT + 8 * i
            self.cf[at : at + 3] = row[0:3]
            self.cf[at + 3 : at + 6] = row[29:32]
        self.cot[...] = self.cf[...].astype(BF16)
        self.branch[...] = (self.cf[...] * w.layer[...]).astype(BF16)
        self.cot_t[...] = self.cot[...].T
        rest = slice(OUT_PIX, OUT_PAD)
        none = jnp.zeros((OUT_PAD - OUT_PIX, C), BF16)
        self.scaled[rest] = none
        for h in range(4):
            self.hid[rest, 256 * h : 256 * h + 256] = none
            self.pg[rest, 256 * h : 256 * h + 256] = none

    def depthwise(self):
        for chans in (slice(0, 128), slice(128, 256)):

            def put_side(i, value):
                self.normed[SIDE_AT + 8 * i : SIDE_AT + 8 * i + 8, chans] = value

            convolve(lambda b, i: self.fs[b, i, :, chans], self.w.taps, chans, INNER, put_side)
            for first, at in ((0, 0), (S - 3, EDGE)):
                for j in range(0, S, 8):

                    def put(i, value):
                        self.normed[at + S * i + j : at + S * i + j + 8, chans] = value

                    convolve(
                        lambda b, i: self.fb[b, first + i, j : j + 8, chans],
                        self.w.taps, chans, 3, put,
                    )

    def norm(self):
        w = self.w
        for at in range(0, OUT_PIX, 80):
            rows = slice(at, at + 80)
            normed, inverse = normalise(self.normed[rows])
            self.inv[rows] = jnp.broadcast_to(inverse, (80, 128))
            self.normed[rows] = normed
            self.scaled[rows] = (normed * w.gain[...]).astype(BF16)
        self.scaled_t[...] = self.scaled[...].T

    def products(self, h):
        part = slice(256 * h, 256 * h + 256)
        self.pre[h % 2] = dot(self.scaled[0:OUT_PIX], self.w.w_in[:, part])
        self.hg[h % 2] = dot(self.branch[0:OUT_PIX], self.w.w_out_t[:, part])

    def hidden(self):
        self.products(0)
        for h in range(4):
            if h < 3:
                self.products(h + 1)
            part = slice(256 * h, 256 * h + 256)
            for at in range(0, OUT_PIX, 16):
                rows = slice(at, at + 16)
                value, slope = gelu_and_slope(self.pre[h % 2, rows])
                self.hid[rows, part] = value.astype(BF16)
                self.pg[rows, part] = (self.hg[h % 2, rows] * slope).astype(BF16)

    def out_grad(self, gacc, big):
        w = self.w
        scale = jnp.zeros((1, C), F32)
        for h in range(4):
            part = slice(256 * h, 256 * h + 256)
            g = (gacc[:, part] + dot(self.cot_t[...], self.hid[:, part])).T
            big[part] = (g * w.layer[...]).astype(BF16)
            scale += jnp.sum(g * w.w_out[part].astype(F32), axis=0, keepdims=True)
        return scale

    def in_grad(self, iacc, big):
        for h in range(4):
            part = slice(256 * h, 256 * h + 256)
            total = iacc[:, part] + dot(self.scaled_t[...], self.pg[:, part])
            big[HID + 256 * h : HID + 256 * h + 256] = total.astype(BF16)

    def scaled_grad(self):
        self.sg[...] = dot(self.pg[0:OUT_PIX], self.w.w_in_t[...])

    def backward(self, gain_acc):
        total = gain_acc[...]
        for at in range(0, OUT_PIX, 80):
            rows = slice(at, at + 80)
            normed = self.normed[rows]
            sg = self.sg[rows]
            total += jnp.sum((sg * normed).reshape(10, 8, C), axis=0)
            self.normed[rows] = norm_backward(sg, normed, self.inv[rows], self.w.gain[...])
        return jnp.sum(total, axis=0, keepdims=True)

    def kernel_grad(self, kg):
        for chans in (slice(0, 128), slice(128, 256)):
            d = [self.normed[SIDE_AT + 8 * i : SIDE_AT + 8 * i + 8, chans] for i in range(INNER)]
            correlate(lambda b, i: self.fs[b, i, :, chans], d, kg, chans)
            for b in range(7):
                acc = [None] * 7
                for first, at in ((0, 0), (S - 3, EDGE)):
                    for j in range(0, S, 8):
                        d = [
                            self.normed[at + S * i + j : at + S * i + j + 8, chans]
                            for i in range(3)
                        ]
                        for i in range(9):
                            f = self.fb[b, first + i, j : j + 8, chans]
                            for a in range(7):
                                if 0 <= i - a < 3:
                                    term = f * d[i - a]
                                    acc[a] = term if acc[a] is None else acc[a] + term
                for a in range(7):
                    kg[7 * a + b, :, chans] += acc[a]


class Weights:
    def __init__(self, bufs):
        (self.taps, self.taps_in, self.gain, self.layer, self.w_in, self.w_in_t, self.w_out,
         self.w_out_t, self.cot) = bufs


def weight_scratch():
    return [
        pltpu.VMEM((49, C), F32),
        pltpu.VMEM((49, C), BF16),
        pltpu.VMEM((1, C), F32),
        pltpu.VMEM((1, C), F32),
        pltpu.VMEM((C, HID), BF16),
        pltpu.VMEM((HID, C), BF16),
        pltpu.VMEM((HID, C), BF16),
        pltpu.VMEM((C, HID), BF16),
        pltpu.VMEM((PIX, C), BF16),
    ]


def inside_scratch():
    return [
        pltpu.VMEM((INNER, S, C), F32),
        pltpu.VMEM((IN_PIX, 128), F32),
        pltpu.VMEM((IN_PAD, C), BF16),
        pltpu.VMEM((IN_PAD, C), BF16),
        pltpu.VMEM((IN_PIX, C), BF16),
        pltpu.VMEM((C, IN_PAD), BF16),
        pltpu.VMEM((C, IN_PAD), BF16),
        pltpu.VMEM((IN_PIX, 256), F32),
        pltpu.VMEM((IN_PIX, 256), F32),
        pltpu.VMEM((IN_PAD, 256), BF16),
        pltpu.VMEM((IN_PAD, HID), BF16),
        pltpu.VMEM((IN_PIX, C), F32),
    ]


def border_scratch():
    return [
        pltpu.VMEM((OUT_PIX, C), F32),
        pltpu.VMEM((OUT_PIX, 128), F32),
        pltpu.VMEM((OUT_PAD, C), BF16),
        pltpu.VMEM((OUT_PAD, C), BF16),
        pltpu.VMEM((OUT_PAD, C), BF16),
        pltpu.VMEM((C, OUT_PAD), BF16),
        pltpu.VMEM((C, OUT_PAD), BF16),
        pltpu.VMEM((2, OUT_PIX, 256), F32),
        pltpu.VMEM((2, OUT_PIX, 256), F32),
        pltpu.VMEM((OUT_PAD, HID), BF16),
        pltpu.VMEM((OUT_PAD, HID), BF16),
        pltpu.VMEM((OUT_PIX, C), F32),
        pltpu.VMEM((OUT_PAD, C), F32),
    ]


FAR_FIRST = (4, 3, 5, 2, 6, 1, 7)


def added(first, rest, count):
    total = first.astype(F32)
    for k in range(count):
        total += rest[k].astype(F32)
    return total


class OutSum:
    def __init__(self, net, me, peers, big, bufs):
        self.net, self.me, self.peers, self.big = net, me, peers, big
        self.r0, self.s1, self.r1, self.s2, self.r2, self.s3, self.r3, self.fin = bufs

    def start(self):
        half = pl.ds(pl.multiple_of((1 - self.me.core) * 512, 512), 512)
        self.c0 = self.net.send(self.big.at[half], self.r0, self.peers.mate)

    def over_z(self):
        self.c0.wait_recv()
        own = self.big[pl.ds(pl.multiple_of(self.me.core * 512, 512), 512)]
        self.s1[...] = added(own, [self.r0[...]], 1).astype(BF16).reshape(NZ, 64, C)
        z = self.me.z
        self.c1 = [
            self.net.send(self.s1.at[lax.rem(z + k, NZ)], self.r1.at[k - 1], self.peers.z[k - 1])
            for k in FAR_FIRST
        ]

    def over_x(self):
        for copy in self.c1:
            copy.wait_recv()
        total = added(self.s1[self.me.z], self.r1, NZ - 1)
        self.s2[...] = total.astype(BF16).reshape(NX, 16, C)
        x = self.me.x
        self.c2 = [
            self.net.send(self.s2.at[lax.rem(x + k, NX)], self.r2.at[k - 1], self.peers.x[k - 1])
            for k in (2, 1, 3)
        ]

    def over_y(self):
        for copy in self.c2:
            copy.wait_recv()
        self.s3[...] = added(self.s2[self.me.x], self.r2, NX - 1).astype(BF16)
        y = self.me.y
        self.r3[y] = self.s3[...]
        self.c3 = [self.net.send(self.s3, self.r3.at[y], self.peers.y[k - 1]) for k in FAR_FIRST]

    def back_x(self):
        for copy in self.c3:
            copy.wait_recv()
        me = self.me
        total = added(self.r3[0], [self.r3[k] for k in range(1, NY)], NY - 1)
        self.fin[me.core, me.z, me.x] = total.astype(BF16)
        mine = self.fin.at[me.core, me.z, me.x]
        self.c4 = [self.net.send(mine, mine, self.peers.x[k - 1]) for k in (2, 1, 3)]

    def back_z(self):
        for copy in self.c4:
            copy.wait_recv()
        mine = self.fin.at[self.me.core, self.me.z]
        self.c5 = [self.net.send(mine, mine, self.peers.z[k - 1]) for k in FAR_FIRST]

    def back_core(self):
        for copy in self.c5:
            copy.wait_recv()
        mine = self.fin.at[self.me.core]
        self.c6 = self.net.send(mine, mine, self.peers.mate)

    def finish(self):
        self.c6.wait_recv()
        return self.fin[...].reshape(HID, C)


class InSum:
    def __init__(self, net, me, peers, big, bufs):
        self.net, self.me, self.peers, self.big = net, me, peers, big
        self.r0, self.s1, self.r1, self.s2, self.r2, self.s3, self.r3, self.fin = bufs

    def start(self):
        half = pl.ds(pl.multiple_of(HID + (1 - self.me.core) * 512, 512), 512)
        self.c0 = self.net.send(self.big.at[half], self.r0, self.peers.mate)

    def over_x(self):
        self.c0.wait_recv()
        own = self.big[pl.ds(pl.multiple_of(HID + self.me.core * 512, 512), 512)]
        self.s1[...] = added(own, [self.r0[...]], 1).astype(BF16).reshape(NX, 128, C)
        x = self.me.x
        self.c1 = [
            self.net.send(self.s1.at[lax.rem(x + k, NX)], self.r1.at[k - 1], self.peers.x[k - 1])
            for k in (2, 1, 3)
        ]

    def over_y(self):
        for copy in self.c1:
            copy.wait_recv()
        total = added(self.s1[self.me.x], self.r1, NX - 1)
        self.s2[...] = total.astype(BF16).reshape(NY, 16, C)
        y = self.me.y
        self.c2 = [
            self.net.send(self.s2.at[lax.rem(y + k, NY)], self.r2.at[k - 1], self.peers.y[k - 1])
            for k in FAR_FIRST
        ]

    def over_z(self):
        for copy in self.c2:
            copy.wait_recv()
        self.s3[...] = added(self.s2[self.me.y], self.r2, NY - 1).astype(BF16)
        z = self.me.z
        self.r3[z] = self.s3[...]
        self.c3 = [self.net.send(self.s3, self.r3.at[z], self.peers.z[k - 1]) for k in FAR_FIRST]

    def back_y(self):
        for copy in self.c3:
            copy.wait_recv()
        me = self.me
        total = added(self.r3[0], [self.r3[k] for k in range(1, NZ)], NZ - 1)
        self.fin[me.core, me.x, me.y] = total.astype(BF16)
        mine = self.fin.at[me.core, me.x, me.y]
        self.c4 = [self.net.send(mine, mine, self.peers.y[k - 1]) for k in FAR_FIRST]

    def back_x(self):
        for copy in self.c4:
            copy.wait_recv()
        mine = self.fin.at[self.me.core, self.me.x]
        self.c5 = [self.net.send(mine, mine, self.peers.x[k - 1]) for k in (2, 1, 3)]

    def back_core(self):
        for copy in self.c5:
            copy.wait_recv()
        mine = self.fin.at[self.me.core]
        self.c6 = self.net.send(mine, mine, self.peers.mate)

    def finish(self):
        self.c6.wait_recv()
        return self.fin[...].reshape(HID, C)


class SmallSum:
    def __init__(self, net, me, peers, small, bufs):
        self.net, self.me, self.peers, self.small = net, me, peers, small
        self.r0, self.s1, self.r1, self.s2, self.r2, self.s3, self.r3, self.fin = bufs

    def start(self):
        half = pl.ds(pl.multiple_of((1 - self.me.core) * 32, 32), 32)
        self.c0 = self.net.send(self.small.at[half], self.r0, self.peers.mate)

    def over_x(self):
        self.c0.wait_recv()
        own = self.small[pl.ds(pl.multiple_of(self.me.core * 32, 32), 32)]
        self.s1[...] = (own + self.r0[...]).reshape(NX, 8, C)
        x = self.me.x
        self.c1 = [
            self.net.send(self.s1.at[lax.rem(x + k, NX)], self.r1.at[k - 1], self.peers.x[k - 1])
            for k in (2, 1, 3)
        ]

    def over_y(self):
        for copy in self.c1:
            copy.wait_recv()
        self.s2[...] = added(self.s1[self.me.x], self.r1, NX - 1)
        y = self.me.y
        self.r2[y] = self.s2[...]
        self.c2 = [self.net.send(self.s2, self.r2.at[y], self.peers.y[k - 1]) for k in FAR_FIRST]

    def over_z(self):
        for copy in self.c2:
            copy.wait_recv()
        self.s3[...] = jnp.sum(self.r2[...], axis=0)
        z = self.me.z
        self.r3[z] = self.s3[...]
        self.c3 = [self.net.send(self.s3, self.r3.at[z], self.peers.z[k - 1]) for k in FAR_FIRST]

    def back_x(self):
        for copy in self.c3:
            copy.wait_recv()
        me = self.me
        self.fin[me.core, me.x] = jnp.sum(self.r3[...], axis=0)
        mine = self.fin.at[me.core, me.x]
        self.c4 = [self.net.send(mine, mine, self.peers.x[k - 1]) for k in (2, 1, 3)]

    def back_core(self):
        for copy in self.c4:
            copy.wait_recv()
        mine = self.fin.at[self.me.core]
        self.c5 = self.net.send(mine, mine, self.peers.mate)

    def finish(self):
        self.c5.wait_recv()
        return self.fin[...].reshape(64, C)


class Peers:
    def __init__(self, me):
        self.mate = me.at(core=1 - me.core)
        self.x = [me.at(x=lax.rem(me.x + k, NX)) for k in range(1, NX)]
        self.y = [me.at(y=lax.rem(me.y + k, NY)) for k in range(1, NY)]
        self.z = [me.at(z=lax.rem(me.z + k, NZ)) for k in range(1, NZ)]

    def all(self):
        return [self.mate] + self.x + self.y + self.z


SUM_COPIES = (1 + 7 + 3 + 7 + 3 + 7 + 1) + (1 + 3 + 7 + 7 + 7 + 3 + 1) + (1 + 3 + 7 + 7 + 3 + 1)


def sum_scratch():
    return [
        pltpu.VMEM((512, C), BF16),
        pltpu.VMEM((NZ, 64, C), BF16),
        pltpu.VMEM((NZ - 1, 64, C), BF16),
        pltpu.VMEM((NX, 16, C), BF16),
        pltpu.VMEM((NX - 1, 16, C), BF16),
        pltpu.VMEM((16, C), BF16),
        pltpu.VMEM((NY, 16, C), BF16),
        pltpu.VMEM((2, NZ, NX, 16, C), BF16),
        pltpu.VMEM((512, C), BF16),
        pltpu.VMEM((NX, 128, C), BF16),
        pltpu.VMEM((NX - 1, 128, C), BF16),
        pltpu.VMEM((NY, 16, C), BF16),
        pltpu.VMEM((NY - 1, 16, C), BF16),
        pltpu.VMEM((16, C), BF16),
        pltpu.VMEM((NZ, 16, C), BF16),
        pltpu.VMEM((2, NX, NY, 16, C), BF16),
        pltpu.VMEM((32, C), F32),
        pltpu.VMEM((NX, 8, C), F32),
        pltpu.VMEM((NX - 1, 8, C), F32),
        pltpu.VMEM((8, C), F32),
        pltpu.VMEM((NY, 8, C), F32),
        pltpu.VMEM((8, C), F32),
        pltpu.VMEM((NZ, 8, C), F32),
        pltpu.VMEM((2, NX, 8, C), F32),
    ]


def sum_sums(outs, ins, smalls, kg_out, gain_out, scale_out, in_out, out_out):
    smalls.over_x()
    smalls.over_y()
    ins.over_y()
    outs.over_x()
    smalls.over_z()
    ins.over_z()
    outs.over_y()
    smalls.back_x()
    ins.back_y()
    outs.back_x()
    smalls.back_core()
    outs.back_z()
    ins.back_x()
    rows = smalls.finish()
    kg_out[...] = rows[0:49]
    gain_out[...] = rows[49:50]
    scale_out[...] = rows[50:51]
    ins.back_core()
    outs.back_core()
    rows = ins.finish()
    for q in range(HID // C):
        in_out[:, 256 * q : 256 * q + 256] = rows[256 * q : 256 * q + 256]
    out_out[...] = outs.finish()


def shared_scratch():
    return [
        pltpu.SMEM((16, 8), jnp.int32),
        pltpu.SMEM((16, 8), jnp.int32),
        pltpu.VMEM((S, S, C), BF16),
        pltpu.VMEM((S, S, C), F32),
        pltpu.VMEM((ROWS, PITCH, C), F32),
        pltpu.VMEM((7, ROWS, S, C), F32),
        pltpu.VMEM((7, S, 8, C), F32),
        pltpu.VMEM((4, 3, S, C), BF16),
        pltpu.VMEM((4, 16, C), BF16),
        pltpu.VMEM((4, 16, C), F32),
        pltpu.VMEM((C, HID), F32),
        pltpu.VMEM((C, HID), F32),
        pltpu.VMEM((49, 8, C), F32),
        pltpu.VMEM((8, C), F32),
        pltpu.VMEM((2 * HID, C), BF16),
        pltpu.VMEM((64, C), F32),
    ]


def split_refs(refs, *lists):
    refs = list(refs)
    parts = []
    for scratch in lists:
        parts.append(refs[: len(scratch)])
        refs = refs[len(scratch) :]
    return parts + [refs]


def block_kernel(
    ids_in, codes_in, x_in, cot_in, taps_in, gain_in, layer_in, w_in_in, w_out_in,
    kg_out, gain_out, scale_out, in_out, out_out, *rest,
):
    shared, weights, rims, inner, outer, sums, sems = split_refs(
        rest, shared_scratch(), weight_scratch(), rim_scratch(), inside_scratch(),
        border_scratch(), sum_scratch(),
    )
    ids, codes, xb, xf, fr, fb, fs, sides, corners, cf, gacc, iacc, kg, gain_acc, big, small = shared
    ss, rs, ls = sems
    w = Weights(weights)
    me = Place()
    peers = Peers(me)
    along_y, along_x = rim_partners(me)
    partners = peers.all() + along_y

    barrier = pltpu.get_barrier_semaphore()
    for device in partners:
        pl.semaphore_signal(barrier, inc=1, device_id=device, device_id_type=MESH)
    loads = [
        pltpu.make_async_copy(src, dst, ls.at[i])
        for i, (src, dst) in enumerate(
            (
                (x_in, xb), (ids_in, ids), (codes_in, codes), (taps_in, w.taps_in),
                (gain_in, w.gain), (layer_in, w.layer), (w_in_in, w.w_in), (w_out_in, w.w_out),
                (cot_in, w.cot),
            )
        )
    ]
    for load in loads:
        load.start()
    loads[0].wait()
    own_strips(xb, xf, rims[0], rims[6], me)
    pl.semaphore_wait(barrier, len(partners))

    net = Copies(ss, rs)
    by_y, by_x = both_rims(net, me, ids, codes, along_y, along_x, rims[:6], rims[6:])
    by_y.gather()
    by_x.gather()
    for load in loads[1:]:
        load.wait()

    inside = Inside(w, fb, inner)
    border = Border(w, fb, fs, outer)
    frame_inside(xf, fr)
    shift_rows(fr, fb, 3, S)
    w.taps[...] = w.taps_in[...].astype(F32)
    by_x.choose()
    inside.depthwise()
    w.w_out_t[...] = w.w_out[...].T
    w.w_in_t[...] = w.w_in[...].T
    inside.norm()
    by_y.choose()
    border.cotangent()
    for h in range(4):
        inside.hidden(h, gacc, iacc)
    inside.backward(gain_acc)
    kg[...] = jnp.zeros_like(kg)
    inside.kernel_grad(kg)

    by_y.take(sides, corners, slice(0, HALF), me.space)
    by_x.take(sides, corners, slice(HALF, C), me.space)
    frame_rims(sides, corners, fr, cf)
    shift_rows(fr, fb, 0, 9)
    shift_rows(fr, fb, S - 3, 9)
    shift_sides(fr, fs)
    border.depthwise()
    border.norm()
    border.hidden()
    outs = OutSum(net, me, peers, big, sums[0:8])
    ins = InSum(net, me, peers, big, sums[8:16])
    smalls = SmallSum(net, me, peers, small, sums[16:24])
    scale = border.out_grad(gacc, big)
    outs.start()
    border.in_grad(iacc, big)
    ins.start()
    border.scaled_grad()
    outs.over_z()
    ins.over_x()
    gain = border.backward(gain_acc)
    border.kernel_grad(kg)
    small[0:49] = jnp.sum(kg[...], axis=1)
    small[49:50] = gain
    small[50:51] = scale
    small[51:64] = jnp.zeros((13, C), F32)
    smalls.start()
    sum_sums(outs, ins, smalls, kg_out, gain_out, scale_out, in_out, out_out)
    net.finish()


def block_grads(neighbours, codes, tile, cot, kernel, ln_gain, layer_scale, w_in, w_out):
    vmem = pl.BlockSpec(memory_space=pltpu.VMEM)
    copies = RIM_COPIES + SUM_COPIES
    return pl.pallas_call(
        block_kernel,
        out_shape=(
            jax.ShapeDtypeStruct((49, C), F32),
            jax.ShapeDtypeStruct((1, C), F32),
            jax.ShapeDtypeStruct((1, C), F32),
            jax.ShapeDtypeStruct((C, HID), BF16),
            jax.ShapeDtypeStruct((HID, C), BF16),
        ),
        in_specs=[pl.BlockSpec(memory_space=pl.ANY)] * 9,
        out_specs=(vmem,) * 5,
        scratch_shapes=shared_scratch() + weight_scratch() + rim_scratch() + inside_scratch()
        + border_scratch() + sum_scratch()
        + [pltpu.SemaphoreType.DMA((copies,))] * 2 + [pltpu.SemaphoreType.DMA((9,))],
        compiler_params=pltpu.CompilerParams(
            collective_id=0, has_side_effects=True, vmem_limit_bytes=60 * 2**20
        ),
    )(
        neighbours, codes, tile, cot, kernel, ln_gain.reshape(1, C), layer_scale.reshape(1, C),
        w_in, w_out,
    )


def on_device(state, cotangent, kernel, ln_gain, w_in, w_out, layer_scale, neighbours, codes):
    kernel_grad, gain_grad, scale_grad, in_grad, out_grad = block_grads(
        neighbours, codes, state.reshape(S, S, C), cotangent.reshape(PIX, C), kernel, ln_gain,
        layer_scale, w_in, w_out,
    )
    return (kernel_grad, gain_grad.reshape(C), scale_grad.reshape(C), in_grad, out_grad)


def solution(mesh):
    placed = (P("dp", "space", None, None, None),) * 2 + (P(),) * 7
    return jax.shard_map(
        on_device, mesh=mesh, in_specs=placed, out_specs=(P(),) * 5, check_vma=False
    )
```

time: 281 us -> 86.8 us (0.31)
  blocking collectives: 117 us -> 0 us
  waiting for transfers between devices: 81.3 us -> 0 us
  Pallas kernels: 0 us -> 78.5 us
  other arithmetic: 32.3 us -> 0 us
  local copies, waits for them, and re-layouts: 24.8 us -> 7.44 us
  between operations: 14.6 us -> 0.66 us
  matrix products: 10.3 us -> 0 us
    psum x1 -> x0, blocking collectives: 117 us -> none  [on_device(): lax.psum((kernel_grad, gain_grad, scale_grad, in_grad, out_grad), ('dp',...]
    all_gather x1 -> x0, waiting for transfers between devices: 81.3 us -> none  [on_device(): lax.all_gather(as_sent(strips), 'space', axis=0, tiled=True)]
    pallas_call x0 -> x1, Pallas kernels: none -> 78.5 us  [block_grads(): pl.pallas_call(block_kernel, out_shape=(jax.ShapeDtypeStruct((49, C), F32...]
    reduce_sum x5 -> x0, other arithmetic: 19.3 us -> none  [the longest x3 9.46 us: block_grads(): kernel_rows.append(jnp.sum(depth_grad * window, axis=(0, 1, 2)))]
    dot_general x6 -> x0, matrix products: 10.3 us -> none  [the longest x2 4.86 us: inner_cols(): lax.dot_general(left, right, (((1,), (1,)), ((), ())), preferred_element_...]
    another operation x7 -> x0, other arithmetic: 9.38 us -> none
    rev x6 -> x0, local copies, waits for them, and re-layouts: 7.76 us -> none  [the longest x3 3.86 us: build_frame(): turned = jnp.rot90(frame, turn, axes=(0, 1))]
    scatter x8 -> x0, local copies, waits for them, and re-layouts: 7.07 us -> none  [build_frame(): turned.at[0:3, 3:-3].set(pieces[turn]).at[0:3, 0:3].set(blocks[turn])]
  transfers between devices with their start and end apart: 1 -> 0, of which waited for: 1 -> 0; matrix products, arithmetic and copies ran while one was open for 1% -> 0% of each run, Pallas kernels for 0% -> 0%
where the time goes in v2:
time: 86.8 us; the launch traced here: 86.6 us
  Pallas kernels  78.5 us (90%)
  local copies, waits for them, and re-layouts  7.44 us (9%)
    pallas_call x1, Pallas kernels, block_grads(): pl.pallas_call(block_kernel, out_shape=(jax.ShapeDtypeStruct((49, C), F32...  78.5 us
    unnamed x17, local copies, waits for them, and re-layouts  7.44 us

profile of v2, /device:TPU:1, one launch (start us, length us, event | category | flops | bytes accessed | tf_op | source)
XLA Modules:
  0.0 86.6 jit_solution(15107877623285115563)
XLA Ops:
  0.6 0.0 copy-start.1
  0.6 0.7 copy-done.1
  1.3 0.0 copy-start.2
  1.3 0.7 copy.14.ids_in
  2.0 0.0 copy-done.2
  2.0 0.7 copy.15.codes_in
  2.7 78.5 %shard_map.128 = (f32[49,256]{1,0:T(8,128)}, f32[1,256]{1,0:T(1,128)}, f32[1,256]{1,0:T(1,128)}, bf16[256,1024]{1,0:T(8,128)(2,1)}, bf16[1024,256]{1,0:T(8,128)(2,1)}) custom-call(s32[16,8]{1,0:T(8,128)} %copy.14.ids_in, s32[16,8]{1,0:T(8,128)} %copy.15.codes_in, bf16[32,32,256]{2,1,0:T(8,128)(2,1)} %bitcast.6, bf16[1024,256]{1,0:T(8,128)(2,1)} %bitcast.7, ...), custom_call_target="tpu_custom_call" | custom-call | tf_op jit(solution)/shard_map/pallas_call | solution.py:970
  81.1 0.0 copy-start.4
  81.2 1.4 %copy.21 = f32[49,256]{1,0:T(8,128)} copy(f32[49,256]{1,0:T(8,128)} %get-tuple-element.20) | data formatting | bytes 100352
  82.6 0.0 copy-done.4
  82.6 0.0 copy-start.3
  82.6 0.6 copy.22
  83.2 0.1 copy-done.3
  83.3 0.6 copy.23
  83.8 0.0 copy-start
  83.8 1.9 %copy.24 = bf16[256,1024]{1,0:T(8,128)(2,1)} copy(bf16[256,1024]{1,0:T(8,128)(2,1)} %get-tuple-element.23) | data formatting | bytes 1048576
  85.8 0.0 copy-done
  85.8 0.8 copy.25
Async XLA Ops:
  0.6 0.7 copy-start.1
  1.3 0.7 copy-start.2
  81.1 1.5 %copy-start.4 = (f32[1,256]{1,0:T(1,128)S(1)}, f32[1,256]{1,0:T(1,128)}, u32[]{:S(2)}) copy-start(f32[1,256]{1,0:T(1,128)} %get-tuple-element.11) | copy-start | bytes 3076
  82.6 0.7 copy-start.3
  83.8 1.9 %copy-start = (bf16[1024,256]{1,0:T(8,128)(2,1)S(1)}, bf16[1024,256]{1,0:T(8,128)(2,1)}, u32[]{:S(2)}) copy-start(bf16[1024,256]{1,0:T(8,128)(2,1)} %get-tuple-element.24) | copy-start | bytes 1572868

commit v3 on v2

--- a/solution.py
+++ b/solution.py
@@ -118,8 +118,8 @@
         for k in (2, 1, 3, 0):
             target = self.tile_at(lax.rem(at + k, 4))
             for s in range(8):
-                row, _ = self.split(jnp.maximum(self.ids[target, s], 0))
-                e = self.codes[target, s]
+                row, _ = self.split(jnp.maximum(self.ids[s, target], 0))
+                e = self.codes[s, target]
                 if s < 4:
                     piece = self.gath[row, e]
                     if k:
@@ -143,7 +143,7 @@
         for copy in self.second:
             copy.wait_recv()
         for s in range(8):
-            n = self.ids[space, s]
+            n = self.ids[s, space]
             _, col = self.split(jnp.maximum(n, 0))
             if s < 4:
                 sides[s, :, :, chans] = self.in_s[col, s]
@@ -654,7 +654,6 @@
 
     def finish(self):
         self.c6.wait_recv()
-        return self.fin[...].reshape(HID, C)
 
 
 class InSum:
@@ -718,7 +717,6 @@
 
     def finish(self):
         self.c6.wait_recv()
-        return self.fin[...].reshape(HID, C)
 
 
 class SmallSum:
@@ -772,7 +770,6 @@
 
     def finish(self):
         self.c5.wait_recv()
-        return self.fin[...].reshape(64, C)
 
 
 class Peers:
@@ -798,7 +795,6 @@
         pltpu.VMEM((NX - 1, 16, C), BF16),
         pltpu.VMEM((16, C), BF16),
         pltpu.VMEM((NY, 16, C), BF16),
-        pltpu.VMEM((2, NZ, NX, 16, C), BF16),
         pltpu.VMEM((512, C), BF16),
         pltpu.VMEM((NX, 128, C), BF16),
         pltpu.VMEM((NX - 1, 128, C), BF16),
@@ -806,7 +802,6 @@
         pltpu.VMEM((NY - 1, 16, C), BF16),
         pltpu.VMEM((16, C), BF16),
         pltpu.VMEM((NZ, 16, C), BF16),
-        pltpu.VMEM((2, NX, NY, 16, C), BF16),
         pltpu.VMEM((32, C), F32),
         pltpu.VMEM((NX, 8, C), F32),
         pltpu.VMEM((NX - 1, 8, C), F32),
@@ -814,11 +809,10 @@
         pltpu.VMEM((NY, 8, C), F32),
         pltpu.VMEM((8, C), F32),
         pltpu.VMEM((NZ, 8, C), F32),
-        pltpu.VMEM((2, NX, 8, C), F32),
     ]
 
 
-def sum_sums(outs, ins, smalls, kg_out, gain_out, scale_out, in_out, out_out):
+def sum_sums(outs, ins, smalls):
     smalls.over_x()
     smalls.over_y()
     ins.over_y()
@@ -832,22 +826,17 @@
     smalls.back_core()
     outs.back_z()
     ins.back_x()
-    rows = smalls.finish()
-    kg_out[...] = rows[0:49]
-    gain_out[...] = rows[49:50]
-    scale_out[...] = rows[50:51]
+    smalls.finish()
     ins.back_core()
     outs.back_core()
-    rows = ins.finish()
-    for q in range(HID // C):
-        in_out[:, 256 * q : 256 * q + 256] = rows[256 * q : 256 * q + 256]
-    out_out[...] = outs.finish()
+    ins.finish()
+    outs.finish()
 
 
 def shared_scratch():
     return [
-        pltpu.SMEM((16, 8), jnp.int32),
-        pltpu.SMEM((16, 8), jnp.int32),
+        pltpu.SMEM((8, 16), jnp.int32),
+        pltpu.SMEM((8, 16), jnp.int32),
         pltpu.VMEM((S, S, C), BF16),
         pltpu.VMEM((S, S, C), F32),
         pltpu.VMEM((ROWS, PITCH, C), F32),
@@ -876,7 +865,7 @@
 
 def block_kernel(
     ids_in, codes_in, x_in, cot_in, taps_in, gain_in, layer_in, w_in_in, w_out_in,
-    kg_out, gain_out, scale_out, in_out, out_out, *rest,
+    out_fin, in_fin, small_fin, *rest,
 ):
     shared, weights, rims, inner, outer, sums, sems = split_refs(
         rest, shared_scratch(), weight_scratch(), rim_scratch(), inside_scratch(),
@@ -921,14 +910,15 @@
     frame_inside(xf, fr)
     shift_rows(fr, fb, 3, S)
     w.taps[...] = w.taps_in[...].astype(F32)
-    by_x.choose()
     inside.depthwise()
     w.w_out_t[...] = w.w_out[...].T
     w.w_in_t[...] = w.w_in[...].T
+    by_x.choose()
     inside.norm()
+    border.cotangent()
+    inside.hidden(0, gacc, iacc)
     by_y.choose()
-    border.cotangent()
-    for h in range(4):
+    for h in range(1, 4):
         inside.hidden(h, gacc, iacc)
     inside.backward(gain_acc)
     kg[...] = jnp.zeros_like(kg)
@@ -943,9 +933,9 @@
     border.depthwise()
     border.norm()
     border.hidden()
-    outs = OutSum(net, me, peers, big, sums[0:8])
-    ins = InSum(net, me, peers, big, sums[8:16])
-    smalls = SmallSum(net, me, peers, small, sums[16:24])
+    outs = OutSum(net, me, peers, big, sums[0:7] + [out_fin])
+    ins = InSum(net, me, peers, big, sums[7:14] + [in_fin])
+    smalls = SmallSum(net, me, peers, small, sums[14:21] + [small_fin])
     scale = border.out_grad(gacc, big)
     outs.start()
     border.in_grad(iacc, big)
@@ -960,7 +950,7 @@
     small[50:51] = scale
     small[51:64] = jnp.zeros((13, C), F32)
     smalls.start()
-    sum_sums(outs, ins, smalls, kg_out, gain_out, scale_out, in_out, out_out)
+    sum_sums(outs, ins, smalls)
     net.finish()
 
 
@@ -970,14 +960,12 @@
     return pl.pallas_call(
         block_kernel,
         out_shape=(
-            jax.ShapeDtypeStruct((49, C), F32),
-            jax.ShapeDtypeStruct((1, C), F32),
-            jax.ShapeDtypeStruct((1, C), F32),
-            jax.ShapeDtypeStruct((C, HID), BF16),
-            jax.ShapeDtypeStruct((HID, C), BF16),
+            pltpu.VMEM((2, NZ, NX, 16, C), BF16),
+            pltpu.VMEM((2, NX, NY, 16, C), BF16),
+            pltpu.VMEM((2, NX, 8, C), F32),
         ),
         in_specs=[pl.BlockSpec(memory_space=pl.ANY)] * 9,
-        out_specs=(vmem,) * 5,
+        out_specs=(vmem,) * 3,
         scratch_shapes=shared_scratch() + weight_scratch() + rim_scratch() + inside_scratch()
         + border_scratch() + sum_scratch()
         + [pltpu.SemaphoreType.DMA((copies,))] * 2 + [pltpu.SemaphoreType.DMA((9,))],
@@ -990,11 +978,63 @@
     )
 
 
+def hand_over_kernel(
+    out_fin, in_fin, small, kg_out, gain_out, scale_out, in_out, out_out, kg, gain, scale, sems
+):
+    def move(pairs, first):
+        copies = [
+            pltpu.make_async_copy(src, dst, sems.at[first + i])
+            for i, (src, dst) in enumerate(pairs)
+        ]
+        for copy in copies:
+            copy.start()
+        return copies
+
+    parts = [
+        (in_fin.at[pl.ds(256 * q, 256)], in_out.at[:, pl.ds(256 * q, 256)])
+        for q in range(HID // C)
+    ]
+    copies = move([(out_fin, out_out)] + parts, 0)
+    kg[...] = small[0:49]
+    gain[...] = small[49:50]
+    scale[...] = small[50:51]
+    copies += move([(kg, kg_out), (gain, gain_out), (scale, scale_out)], 5)
+    for copy in copies:
+        copy.wait()
+
+
+def hand_over(out_fin, in_fin, small_fin):
+    return pl.pallas_call(
+        hand_over_kernel,
+        out_shape=(
+            jax.ShapeDtypeStruct((49, C), F32),
+            jax.ShapeDtypeStruct((1, C), F32),
+            jax.ShapeDtypeStruct((1, C), F32),
+            jax.ShapeDtypeStruct((C, HID), BF16),
+            jax.ShapeDtypeStruct((HID, C), BF16),
+        ),
+        in_specs=[pl.BlockSpec(memory_space=pltpu.VMEM)] * 3,
+        out_specs=(pl.BlockSpec(memory_space=pl.ANY),) * 5,
+        scratch_shapes=[
+            pltpu.VMEM((49, C), F32),
+            pltpu.VMEM((1, C), F32),
+            pltpu.VMEM((1, C), F32),
+            pltpu.SemaphoreType.DMA((8,)),
+        ],
+        compiler_params=pltpu.CompilerParams(has_side_effects=True),
+    )(
+        pltpu.with_memory_space_constraint(out_fin.reshape(HID, C), pltpu.VMEM),
+        pltpu.with_memory_space_constraint(in_fin.reshape(HID, C), pltpu.VMEM),
+        pltpu.with_memory_space_constraint(small_fin.reshape(64, C), pltpu.VMEM),
+    )
+
+
 def on_device(state, cotangent, kernel, ln_gain, w_in, w_out, layer_scale, neighbours, codes):
-    kernel_grad, gain_grad, scale_grad, in_grad, out_grad = block_grads(
-        neighbours, codes, state.reshape(S, S, C), cotangent.reshape(PIX, C), kernel, ln_gain,
+    sums = block_grads(
+        neighbours.T, codes.T, state.reshape(S, S, C), cotangent.reshape(PIX, C), kernel, ln_gain,
         layer_scale, w_in, w_out,
     )
+    kernel_grad, gain_grad, scale_grad, in_grad, out_grad = hand_over(*sums)
     return (kernel_grad, gain_grad.reshape(C), scale_grad.reshape(C), in_grad, out_grad)
 
 

time: 86.8 us -> 77.4 us (0.89)
  local copies, waits for them, and re-layouts: 7.44 us -> 0 us
  Pallas kernels: 78.5 us -> 76.4 us
    unnamed x17 -> x0, local copies, waits for them, and re-layouts: 7.44 us -> none
    pallas_call x1 -> x2, Pallas kernels: 78.5 us -> 76.4 us  [the longest x1 75.4 us: block_grads(): pl.pallas_call(block_kernel, out_shape=(pltpu.VMEM((2, NZ, NX, 16, C), BF...]
where the time goes in v3:
time: 77.4 us; the launch traced here: 77.2 us
  Pallas kernels  76.4 us (99%)
  between operations  0.8 us (1%)
    pallas_call x1, Pallas kernels, block_grads(): pl.pallas_call(block_kernel, out_shape=(pltpu.VMEM((2, NZ, NX, 16, C), BF...  75.4 us

profile of v3, /device:TPU:1, one launch (start us, length us, event | category | flops | bytes accessed | tf_op | source)
XLA Modules:
  0.0 77.2 jit_solution(13890632054397139728)
XLA Ops:
  0.6 75.4 %shard_map.128 = (bf16[2,8,4,16,256]{4,3,2,1,0:T(8,128)(2,1)S(1)}, bf16[2,4,8,16,256]{4,3,2,1,0:T(8,128)(2,1)S(1)}, f32[2,4,8,256]{3,2,1,0:T(8,128)S(1)}) custom-call(s32[8,16]{1,0:T(8,128)} %bitcast.16, s32[8,16]{1,0:T(8,128)} %bitcast.17, bf16[32,32,256]{2,1,0:T(8,128)(2,1)} %bitcast.14, bf16[1024,256]{1,0:T(8,128)(2,1)} %bitcast.15, ...), custom_call_target="tpu_custom_call" | custom-call | tf_op jit(solution)/shard_map/pallas_call | solution.py:960
  76.0 1.0 %shard_map.129 = (f32[49,256]{1,0:T(8,128)}, f32[1,256]{1,0:T(1,128)}, f32[1,256]{1,0:T(1,128)}, bf16[256,1024]{1,0:T(8,128)(2,1)}, bf16[1024,256]{1,0:T(8,128)(2,1)}) custom-call(bf16[1024,256]{1,0:T(8,128)(2,1)S(1)} %bitcast.11, bf16[1024,256]{1,0:T(8,128)(2,1)S(1)} %bitcast.12, f32[64,256]{1,0:T(8,128)S(1)} %bitcast.13), custom_call_target="tpu_custom_call" | custom-call | tf_op jit(solution)/shard_map/pallas_call | solution.py:1007

commit v4 on v3

--- a/solution.py
+++ b/solution.py
@@ -197,6 +197,9 @@
 
 
 INNER = S - 6
+NORM_ROWS = 13
+NORM_PIX = NORM_ROWS * S
+ACT_ROWS = 208
 IN_PIX = INNER * S
 IN_PAD = 896
 EDGE = 3 * S
@@ -215,38 +218,38 @@
     lax.fori_loop(0, S, one_row, 0)
 
 
-def frame_rims(sides, corners, fr, cf):
+def frame_rims(sides, corners, fr, cf, chans):
     turn = reversal()
     for r in range(3):
-        fr[r, 3 : 3 + S, :] = flip(turn, sides[0, 2 - r]).astype(F32)
-        fr[3 : 3 + S, 35 + r, :] = flip(turn, sides[1, r]).astype(F32)
-        fr[35 + r, 3 : 3 + S, :] = sides[2, r].astype(F32)
-        fr[3 : 3 + S, r, :] = sides[3, 2 - r].astype(F32)
-    cf[...] = corners[...].astype(F32)
+        fr[r, 3 : 3 + S, chans] = flip(turn, sides[0, 2 - r, :, chans]).astype(F32)
+        fr[3 : 3 + S, 35 + r, chans] = flip(turn, sides[1, r, :, chans]).astype(F32)
+        fr[35 + r, 3 : 3 + S, chans] = sides[2, r, :, chans].astype(F32)
+        fr[3 : 3 + S, r, chans] = sides[3, 2 - r, :, chans].astype(F32)
+    cf[:, :, chans] = corners[:, :, chans].astype(F32)
     for i in range(3):
         for j in range(3):
-            fr[i, j, :] = cf[0, 4 * (2 - i) + 2 - j, :]
-            fr[i, 35 + j, :] = cf[1, 4 * j + 2 - i, :]
-            fr[35 + i, 35 + j, :] = cf[2, 4 * i + j, :]
-            fr[35 + i, j, :] = cf[3, 4 * (2 - j) + i, :]
-
-
-def shift_rows(fr, fb, first, count):
+            fr[i, j, chans] = cf[0, 4 * (2 - i) + 2 - j, chans]
+            fr[i, 35 + j, chans] = cf[1, 4 * j + 2 - i, chans]
+            fr[35 + i, 35 + j, chans] = cf[2, 4 * i + j, chans]
+            fr[35 + i, j, chans] = cf[3, 4 * (2 - j) + i, chans]
+
+
+def shift_rows(fr, fb, first, count, chans=slice(0, C)):
     def one_row(i, carry):
         for b in range(7):
-            fb[b, first + i] = fr[first + i, b : b + S, :]
+            fb[b, first + i, :, chans] = fr[first + i, b : b + S, chans]
         return carry
 
     lax.fori_loop(0, count, one_row, 0)
 
 
-def shift_sides(fr, fs):
-    fs[...] = jnp.zeros_like(fs)
+def shift_sides(fr, fs, chans):
+    fs[:, :, :, chans] = jnp.zeros((7, S, 8, HALF), F32)
 
     def one_row(i, carry):
         for b in range(7):
-            fs[b, i, 0:3, :] = fr[3 + i, b : b + 3, :]
-            fs[b, i, 3:6, :] = fr[3 + i, 29 + b : 32 + b, :]
+            fs[b, i, 0:3, chans] = fr[3 + i, b : b + 3, chans]
+            fs[b, i, 3:6, chans] = fr[3 + i, 29 + b : 32 + b, chans]
         return carry
 
     lax.fori_loop(0, S, one_row, 0)
@@ -337,23 +340,24 @@
 
     def norm(self):
         w = self.w
-        col = lax.rem(lax.broadcasted_iota(jnp.int32, (64, C), 0), S)
-        here = (col >= 3) & (col < S - 3)
+        col = lax.rem(lax.broadcasted_iota(jnp.int32, (S, C), 0), S)
+        here = ((col >= 3) & (col < S - 3))[None]
 
         def step(q, carry):
-            rows = pl.ds(q * 2, 2)
-            flat = pl.ds(pl.multiple_of(q * 64, 64), 64)
-            normed, inverse = normalise(self.normed[rows].reshape(64, C))
-            self.inv[flat] = jnp.broadcast_to(inverse, (64, 128))
-            self.normed[rows] = normed.reshape(2, S, C)
+            rows = pl.ds(q * NORM_ROWS, NORM_ROWS)
+            flat = pl.ds(pl.multiple_of(q * NORM_PIX, 32), NORM_PIX)
+            normed, inverse = normalise(self.normed[rows].reshape(NORM_PIX, C))
+            self.inv[flat] = jnp.broadcast_to(inverse, (NORM_PIX, 128))
+            self.normed[rows] = normed.reshape(NORM_ROWS, S, C)
             self.scaled[flat] = (normed * w.gain[...]).astype(BF16)
-            cot = w.cot[pl.ds(pl.multiple_of(3 * S + q * 64, 32), 64)].astype(F32)
-            cot = jnp.where(here, cot, jnp.zeros_like(cot))
+            cot = w.cot[pl.ds(pl.multiple_of(3 * S + q * NORM_PIX, 32), NORM_PIX)].astype(F32)
+            cot = cot.reshape(NORM_ROWS, S, C)
+            cot = jnp.where(here, cot, jnp.zeros_like(cot)).reshape(NORM_PIX, C)
             self.cot[flat] = cot.astype(BF16)
             self.branch[flat] = (cot * w.layer[...]).astype(BF16)
             return carry
 
-        lax.fori_loop(0, INNER // 2, step, 0)
+        lax.fori_loop(0, INNER // NORM_ROWS, step, 0)
         rest = slice(IN_PIX, IN_PAD)
         none = jnp.zeros((IN_PAD - IN_PIX, C), BF16)
         self.scaled[rest] = none
@@ -371,13 +375,13 @@
         self.hg[...] = dot(self.branch[...], w.w_out_t[:, part])
 
         def act(q, carry):
-            rows = pl.ds(pl.multiple_of(q * 32, 32), 32)
+            rows = pl.ds(pl.multiple_of(q * ACT_ROWS, 16), ACT_ROWS)
             value, slope = gelu_and_slope(self.pre[rows])
             self.hid[rows] = value.astype(BF16)
             self.pg[rows, part] = (self.hg[rows] * slope).astype(BF16)
             return carry
 
-        lax.fori_loop(0, IN_PIX // 32, act, 0)
+        lax.fori_loop(0, IN_PIX // ACT_ROWS, act, 0)
         gacc[:, part] = dot(self.cot_t[...], self.hid[...])
         iacc[:, part] = dot(self.scaled_t[...], self.pg[:, part])
 
@@ -386,15 +390,15 @@
         self.sg[...] = dot(self.pg[0:IN_PIX], w.w_in_t[...])
 
         def step(q, total):
-            rows = pl.ds(q * 2, 2)
-            flat = pl.ds(pl.multiple_of(q * 64, 64), 64)
-            normed = self.normed[rows].reshape(64, C)
+            rows = pl.ds(q * NORM_ROWS, NORM_ROWS)
+            flat = pl.ds(pl.multiple_of(q * NORM_PIX, 32), NORM_PIX)
+            normed = self.normed[rows].reshape(NORM_PIX, C)
             sg = self.sg[flat]
             grad = norm_backward(sg, normed, self.inv[flat], w.gain[...])
-            self.normed[rows] = grad.reshape(2, S, C)
-            return total + jnp.sum((sg * normed).reshape(8, 8, C), axis=0)
-
-        gain_acc[...] = lax.fori_loop(0, INNER // 2, step, jnp.zeros((8, C), F32))
+            self.normed[rows] = grad.reshape(NORM_ROWS, S, C)
+            return total + jnp.sum((sg * normed).reshape(NORM_PIX // 8, 8, C), axis=0)
+
+        gain_acc[...] = lax.fori_loop(0, INNER // NORM_ROWS, step, jnp.zeros((8, C), F32))
 
     def kernel_grad(self, kg):
         def step(g, carry):
@@ -432,23 +436,21 @@
             self.hid[rest, 256 * h : 256 * h + 256] = none
             self.pg[rest, 256 * h : 256 * h + 256] = none
 
-    def depthwise(self):
-        for chans in (slice(0, 128), slice(128, 256)):
-
-            def put_side(i, value):
-                self.normed[SIDE_AT + 8 * i : SIDE_AT + 8 * i + 8, chans] = value
-
-            convolve(lambda b, i: self.fs[b, i, :, chans], self.w.taps, chans, INNER, put_side)
-            for first, at in ((0, 0), (S - 3, EDGE)):
-                for j in range(0, S, 8):
-
-                    def put(i, value):
-                        self.normed[at + S * i + j : at + S * i + j + 8, chans] = value
-
-                    convolve(
-                        lambda b, i: self.fb[b, first + i, j : j + 8, chans],
-                        self.w.taps, chans, 3, put,
-                    )
+    def depthwise(self, chans):
+        def put_side(i, value):
+            self.normed[SIDE_AT + 8 * i : SIDE_AT + 8 * i + 8, chans] = value
+
+        convolve(lambda b, i: self.fs[b, i, :, chans], self.w.taps, chans, INNER, put_side)
+        for first, at in ((0, 0), (S - 3, EDGE)):
+            for j in range(0, S, 8):
+
+                def put(i, value):
+                    self.normed[at + S * i + j : at + S * i + j + 8, chans] = value
+
+                convolve(
+                    lambda b, i: self.fb[b, first + i, j : j + 8, chans],
+                    self.w.taps, chans, 3, put,
+                )
 
     def norm(self):
         w = self.w
@@ -460,10 +462,14 @@
             self.scaled[rows] = (normed * w.gain[...]).astype(BF16)
         self.scaled_t[...] = self.scaled[...].T
 
+    def hidden_grad(self):
+        for h in range(4):
+            part = slice(256 * h, 256 * h + 256)
+            self.hg[h] = dot(self.branch[0:OUT_PIX], self.w.w_out_t[:, part])
+
     def products(self, h):
         part = slice(256 * h, 256 * h + 256)
         self.pre[h % 2] = dot(self.scaled[0:OUT_PIX], self.w.w_in[:, part])
-        self.hg[h % 2] = dot(self.branch[0:OUT_PIX], self.w.w_out_t[:, part])
 
     def hidden(self):
         self.products(0)
@@ -475,7 +481,7 @@
                 rows = slice(at, at + 16)
                 value, slope = gelu_and_slope(self.pre[h % 2, rows])
                 self.hid[rows, part] = value.astype(BF16)
-                self.pg[rows, part] = (self.hg[h % 2, rows] * slope).astype(BF16)
+                self.pg[rows, part] = (self.hg[h, rows] * slope).astype(BF16)
 
     def out_grad(self, gacc, big):
         w = self.w
@@ -575,7 +581,7 @@
         pltpu.VMEM((C, OUT_PAD), BF16),
         pltpu.VMEM((C, OUT_PAD), BF16),
         pltpu.VMEM((2, OUT_PIX, 256), F32),
-        pltpu.VMEM((2, OUT_PIX, 256), F32),
+        pltpu.VMEM((4, OUT_PIX, 256), F32),
         pltpu.VMEM((OUT_PAD, HID), BF16),
         pltpu.VMEM((OUT_PAD, HID), BF16),
         pltpu.VMEM((OUT_PIX, C), F32),
@@ -593,82 +599,86 @@
     return total
 
 
-class OutSum:
+CROSS = 384
+CHUNK = CROSS // 8
+PLANE = 256
+PLANE_AT = 2 * CROSS
+
+
+class CrossSum:
+    def __init__(self, net, me, peers, big, base, first, bufs):
+        self.net, self.me, self.big, self.base = net, me, big, base
+        self.peers = peers
+        self.at, self.to = (me.z, peers.z) if first == "z" else (me.y, peers.y)
+        self.other_at, self.other_to = (me.y, peers.y) if first == "z" else (me.z, peers.z)
+        self.r0, self.s1, self.r1, self.s2, self.r2, self.s3, self.r3, self.fin = bufs
+
+    def half(self, core):
+        return pl.ds(pl.multiple_of(self.base + core * CROSS, 128), CROSS)
+
+    def start(self):
+        self.c0 = self.net.send(self.big.at[self.half(1 - self.me.core)], self.r0, self.peers.mate)
+
+    def over_first(self):
+        self.c0.wait_recv()
+        own = self.big[self.half(self.me.core)]
+        self.s1[...] = added(own, [self.r0[...]], 1).astype(BF16).reshape(8, CHUNK, C)
+        self.c1 = [
+            self.net.send(self.s1.at[lax.rem(self.at + k, 8)], self.r1.at[k - 1], self.to[k - 1])
+            for k in FAR_FIRST
+        ]
+
+    def over_x(self):
+        for copy in self.c1:
+            copy.wait_recv()
+        self.s2[...] = added(self.s1[self.at], self.r1, 7).astype(BF16)
+        x = self.me.x
+        self.r2[x] = self.s2[...]
+        self.c2 = [self.net.send(self.s2, self.r2.at[x], self.peers.x[k - 1]) for k in (2, 1, 3)]
+
+    def over_other(self):
+        for copy in self.c2:
+            copy.wait_recv()
+        total = added(self.r2[0], [self.r2[k] for k in range(1, NX)], NX - 1)
+        self.s3[...] = total.astype(BF16)
+        at = self.other_at
+        self.r3[at] = self.s3[...]
+        self.c3 = [self.net.send(self.s3, self.r3.at[at], self.other_to[k - 1]) for k in FAR_FIRST]
+
+    def back_first(self):
+        for copy in self.c3:
+            copy.wait_recv()
+        total = added(self.r3[0], [self.r3[k] for k in range(1, 8)], 7)
+        core = self.me.core
+        self.fin[core, self.at] = total.astype(BF16)
+        mine = self.fin.at[core, self.at]
+        self.c4 = [self.net.send(mine, mine, self.to[k - 1]) for k in FAR_FIRST]
+
+    def back_core(self):
+        for copy in self.c4:
+            copy.wait_recv()
+        mine = self.fin.at[self.me.core]
+        self.c5 = self.net.send(mine, mine, self.peers.mate)
+
+    def finish(self):
+        self.c5.wait_recv()
+
+
+class PlaneSum:
     def __init__(self, net, me, peers, big, bufs):
         self.net, self.me, self.peers, self.big = net, me, peers, big
         self.r0, self.s1, self.r1, self.s2, self.r2, self.s3, self.r3, self.fin = bufs
 
+    def half(self, core):
+        return pl.ds(pl.multiple_of(PLANE_AT + core * PLANE, 256), PLANE)
+
     def start(self):
-        half = pl.ds(pl.multiple_of((1 - self.me.core) * 512, 512), 512)
-        self.c0 = self.net.send(self.big.at[half], self.r0, self.peers.mate)
-
-    def over_z(self):
-        self.c0.wait_recv()
-        own = self.big[pl.ds(pl.multiple_of(self.me.core * 512, 512), 512)]
-        self.s1[...] = added(own, [self.r0[...]], 1).astype(BF16).reshape(NZ, 64, C)
-        z = self.me.z
-        self.c1 = [
-            self.net.send(self.s1.at[lax.rem(z + k, NZ)], self.r1.at[k - 1], self.peers.z[k - 1])
-            for k in FAR_FIRST
-        ]
-
-    def over_x(self):
-        for copy in self.c1:
-            copy.wait_recv()
-        total = added(self.s1[self.me.z], self.r1, NZ - 1)
-        self.s2[...] = total.astype(BF16).reshape(NX, 16, C)
-        x = self.me.x
-        self.c2 = [
-            self.net.send(self.s2.at[lax.rem(x + k, NX)], self.r2.at[k - 1], self.peers.x[k - 1])
-            for k in (2, 1, 3)
-        ]
-
-    def over_y(self):
-        for copy in self.c2:
-            copy.wait_recv()
-        self.s3[...] = added(self.s2[self.me.x], self.r2, NX - 1).astype(BF16)
-        y = self.me.y
-        self.r3[y] = self.s3[...]
-        self.c3 = [self.net.send(self.s3, self.r3.at[y], self.peers.y[k - 1]) for k in FAR_FIRST]
-
-    def back_x(self):
-        for copy in self.c3:
-            copy.wait_recv()
-        me = self.me
-        total = added(self.r3[0], [self.r3[k] for k in range(1, NY)], NY - 1)
-        self.fin[me.core, me.z, me.x] = total.astype(BF16)
-        mine = self.fin.at[me.core, me.z, me.x]
-        self.c4 = [self.net.send(mine, mine, self.peers.x[k - 1]) for k in (2, 1, 3)]
-
-    def back_z(self):
-        for copy in self.c4:
-            copy.wait_recv()
-        mine = self.fin.at[self.me.core, self.me.z]
-        self.c5 = [self.net.send(mine, mine, self.peers.z[k - 1]) for k in FAR_FIRST]
-
-    def back_core(self):
-        for copy in self.c5:
-            copy.wait_recv()
-        mine = self.fin.at[self.me.core]
-        self.c6 = self.net.send(mine, mine, self.peers.mate)
-
-    def finish(self):
-        self.c6.wait_recv()
-
-
-class InSum:
-    def __init__(self, net, me, peers, big, bufs):
-        self.net, self.me, self.peers, self.big = net, me, peers, big
-        self.r0, self.s1, self.r1, self.s2, self.r2, self.s3, self.r3, self.fin = bufs
-
-    def start(self):
-        half = pl.ds(pl.multiple_of(HID + (1 - self.me.core) * 512, 512), 512)
-        self.c0 = self.net.send(self.big.at[half], self.r0, self.peers.mate)
+        self.c0 = self.net.send(self.big.at[self.half(1 - self.me.core)], self.r0, self.peers.mate)
 
     def over_x(self):
         self.c0.wait_recv()
-        own = self.big[pl.ds(pl.multiple_of(HID + self.me.core * 512, 512), 512)]
-        self.s1[...] = added(own, [self.r0[...]], 1).astype(BF16).reshape(NX, 128, C)
+        own = self.big[self.half(self.me.core)]
+        self.s1[...] = added(own, [self.r0[...]], 1).astype(BF16).reshape(NX, 64, C)
         x = self.me.x
         self.c1 = [
             self.net.send(self.s1.at[lax.rem(x + k, NX)], self.r1.at[k - 1], self.peers.x[k - 1])
@@ -678,8 +688,10 @@
     def over_y(self):
         for copy in self.c1:
             copy.wait_recv()
-        total = added(self.s1[self.me.x], self.r1, NX - 1)
-        self.s2[...] = total.astype(BF16).reshape(NY, 16, C)
+        total = added(self.s1[self.me.x], self.r1, NX - 1).astype(BF16)
+        for t in range(NY):
+            rows, cols = 16 * (t // 2), 128 * (t % 2)
+            self.s2[t] = total[rows : rows + 16, cols : cols + 128]
         y = self.me.y
         self.c2 = [
             self.net.send(self.s2.at[lax.rem(y + k, NY)], self.r2.at[k - 1], self.peers.y[k - 1])
@@ -699,24 +711,31 @@
             copy.wait_recv()
         me = self.me
         total = added(self.r3[0], [self.r3[k] for k in range(1, NZ)], NZ - 1)
-        self.fin[me.core, me.x, me.y] = total.astype(BF16)
-        mine = self.fin.at[me.core, me.x, me.y]
+        at = (lax.rem(me.y, 2), me.core, me.x, me.y // 2)
+        self.fin[at] = total.astype(BF16)
+        mine = self.fin.at[at]
         self.c4 = [self.net.send(mine, mine, self.peers.y[k - 1]) for k in FAR_FIRST]
 
     def back_x(self):
         for copy in self.c4:
             copy.wait_recv()
-        mine = self.fin.at[self.me.core, self.me.x]
-        self.c5 = [self.net.send(mine, mine, self.peers.x[k - 1]) for k in (2, 1, 3)]
+        self.c5 = []
+        for k in (2, 1, 3):
+            for half in range(2):
+                mine = self.fin.at[half, self.me.core, self.me.x]
+                self.c5.append(self.net.send(mine, mine, self.peers.x[k - 1]))
 
     def back_core(self):
         for copy in self.c5:
             copy.wait_recv()
-        mine = self.fin.at[self.me.core]
-        self.c6 = self.net.send(mine, mine, self.peers.mate)
+        self.c6 = []
+        for half in range(2):
+            mine = self.fin.at[half, self.me.core]
+            self.c6.append(self.net.send(mine, mine, self.peers.mate))
 
     def finish(self):
-        self.c6.wait_recv()
+        for copy in self.c6:
+            copy.wait_recv()
 
 
 class SmallSum:
@@ -783,25 +802,27 @@
         return [self.mate] + self.x + self.y + self.z
 
 
-SUM_COPIES = (1 + 7 + 3 + 7 + 3 + 7 + 1) + (1 + 3 + 7 + 7 + 7 + 3 + 1) + (1 + 3 + 7 + 7 + 3 + 1)
+SUM_COPIES = (1 + 3 + 7 + 7 + 7 + 6 + 2) + 2 * (1 + 7 + 3 + 7 + 7 + 1) + (1 + 3 + 7 + 7 + 3 + 1)
 
 
 def sum_scratch():
-    return [
-        pltpu.VMEM((512, C), BF16),
-        pltpu.VMEM((NZ, 64, C), BF16),
-        pltpu.VMEM((NZ - 1, 64, C), BF16),
-        pltpu.VMEM((NX, 16, C), BF16),
-        pltpu.VMEM((NX - 1, 16, C), BF16),
-        pltpu.VMEM((16, C), BF16),
-        pltpu.VMEM((NY, 16, C), BF16),
-        pltpu.VMEM((512, C), BF16),
-        pltpu.VMEM((NX, 128, C), BF16),
-        pltpu.VMEM((NX - 1, 128, C), BF16),
-        pltpu.VMEM((NY, 16, C), BF16),
-        pltpu.VMEM((NY - 1, 16, C), BF16),
-        pltpu.VMEM((16, C), BF16),
-        pltpu.VMEM((NZ, 16, C), BF16),
+    cross = [
+        pltpu.VMEM((CROSS, C), BF16),
+        pltpu.VMEM((8, CHUNK, C), BF16),
+        pltpu.VMEM((7, CHUNK, C), BF16),
+        pltpu.VMEM((CHUNK, C), BF16),
+        pltpu.VMEM((NX, CHUNK, C), BF16),
+        pltpu.VMEM((CHUNK, C), BF16),
+        pltpu.VMEM((8, CHUNK, C), BF16),
+    ]
+    return cross * 2 + [
+        pltpu.VMEM((PLANE, C), BF16),
+        pltpu.VMEM((NX, 64, C), BF16),
+        pltpu.VMEM((NX - 1, 64, C), BF16),
+        pltpu.VMEM((NY, 16, 128), BF16),
+        pltpu.VMEM((NY - 1, 16, 128), BF16),
+        pltpu.VMEM((16, 128), BF16),
+        pltpu.VMEM((NZ, 16, 128), BF16),
         pltpu.VMEM((32, C), F32),
         pltpu.VMEM((NX, 8, C), F32),
         pltpu.VMEM((NX - 1, 8, C), F32),
@@ -812,25 +833,29 @@
     ]
 
 
-def sum_sums(outs, ins, smalls):
+def sum_sums(by_z, plane, by_y, smalls):
+    plane.over_y()
     smalls.over_x()
+    by_z.over_x()
+    by_y.over_x()
     smalls.over_y()
-    ins.over_y()
-    outs.over_x()
+    plane.over_z()
+    by_z.over_other()
+    by_y.over_other()
     smalls.over_z()
-    ins.over_z()
-    outs.over_y()
+    plane.back_y()
+    by_z.back_first()
+    by_y.back_first()
     smalls.back_x()
-    ins.back_y()
-    outs.back_x()
+    plane.back_x()
+    by_z.back_core()
     smalls.back_core()
-    outs.back_z()
-    ins.back_x()
+    by_y.back_core()
+    plane.back_core()
     smalls.finish()
-    ins.back_core()
-    outs.back_core()
-    ins.finish()
-    outs.finish()
+    by_z.finish()
+    by_y.finish()
+    plane.finish()
 
 
 def shared_scratch():
@@ -865,7 +890,7 @@
 
 def block_kernel(
     ids_in, codes_in, x_in, cot_in, taps_in, gain_in, layer_in, w_in_in, w_out_in,
-    out_fin, in_fin, small_fin, *rest,
+    fin_z, fin_plane, fin_y, fin_small, *rest,
 ):
     shared, weights, rims, inner, outer, sums, sems = split_refs(
         rest, shared_scratch(), weight_scratch(), rim_scratch(), inside_scratch(),
@@ -913,36 +938,41 @@
     inside.depthwise()
     w.w_out_t[...] = w.w_out[...].T
     w.w_in_t[...] = w.w_in[...].T
+    inside.norm()
     by_x.choose()
-    inside.norm()
     border.cotangent()
-    inside.hidden(0, gacc, iacc)
+    border.hidden_grad()
+    for h in range(3):
+        inside.hidden(h, gacc, iacc)
     by_y.choose()
-    for h in range(1, 4):
+    for h in range(3, 4):
         inside.hidden(h, gacc, iacc)
     inside.backward(gain_acc)
     kg[...] = jnp.zeros_like(kg)
     inside.kernel_grad(kg)
 
-    by_y.take(sides, corners, slice(0, HALF), me.space)
-    by_x.take(sides, corners, slice(HALF, C), me.space)
-    frame_rims(sides, corners, fr, cf)
-    shift_rows(fr, fb, 0, 9)
-    shift_rows(fr, fb, S - 3, 9)
-    shift_sides(fr, fs)
-    border.depthwise()
+    for rim, chans in ((by_y, slice(0, HALF)), (by_x, slice(HALF, C))):
+        rim.take(sides, corners, chans, me.space)
+        frame_rims(sides, corners, fr, cf, chans)
+        shift_rows(fr, fb, 0, 9, chans)
+        shift_rows(fr, fb, S - 3, 9, chans)
+        shift_sides(fr, fs, chans)
+        border.depthwise(chans)
     border.norm()
     border.hidden()
-    outs = OutSum(net, me, peers, big, sums[0:7] + [out_fin])
-    ins = InSum(net, me, peers, big, sums[7:14] + [in_fin])
-    smalls = SmallSum(net, me, peers, small, sums[14:21] + [small_fin])
+    sum_z = CrossSum(net, me, peers, big, 0, "z", sums[0:7] + [fin_z])
+    sum_y = CrossSum(net, me, peers, big, PLANE_AT + 2 * PLANE, "y", sums[7:14] + [fin_y])
+    plane = PlaneSum(net, me, peers, big, sums[14:21] + [fin_plane])
+    smalls = SmallSum(net, me, peers, small, sums[21:28] + [fin_small])
     scale = border.out_grad(gacc, big)
-    outs.start()
+    sum_z.start()
     border.in_grad(iacc, big)
-    ins.start()
+    plane.start()
+    sum_y.start()
     border.scaled_grad()
-    outs.over_z()
-    ins.over_x()
+    sum_z.over_first()
+    plane.over_x()
+    sum_y.over_first()
     gain = border.backward(gain_acc)
     border.kernel_grad(kg)
     small[0:49] = jnp.sum(kg[...], axis=1)
@@ -950,7 +980,7 @@
     small[50:51] = scale
     small[51:64] = jnp.zeros((13, C), F32)
     smalls.start()
-    sum_sums(outs, ins, smalls)
+    sum_sums(sum_z, plane, sum_y, smalls)
     net.finish()
 
 
@@ -960,12 +990,13 @@
     return pl.pallas_call(
         block_kernel,
         out_shape=(
-            pltpu.VMEM((2, NZ, NX, 16, C), BF16),
-            pltpu.VMEM((2, NX, NY, 16, C), BF16),
+            pltpu.VMEM((2, NZ, CHUNK, C), BF16),
+            pltpu.VMEM((2, 2, NX, 4, 16, 128), BF16),
+            pltpu.VMEM((2, NY, CHUNK, C), BF16),
             pltpu.VMEM((2, NX, 8, C), F32),
         ),
         in_specs=[pl.BlockSpec(memory_space=pl.ANY)] * 9,
-        out_specs=(vmem,) * 3,
+        out_specs=(vmem,) * 4,
         scratch_shapes=shared_scratch() + weight_scratch() + rim_scratch() + inside_scratch()
         + border_scratch() + sum_scratch()
         + [pltpu.SemaphoreType.DMA((copies,))] * 2 + [pltpu.SemaphoreType.DMA((9,))],
@@ -979,7 +1010,7 @@
 
 
 def hand_over_kernel(
-    out_fin, in_fin, small, kg_out, gain_out, scale_out, in_out, out_out, kg, gain, scale, sems
+    fin_z, fin_plane, fin_y, small, kg_out, gain_out, scale_out, in_out, out_out, kg, gain, scale, sems
 ):
     def move(pairs, first):
         copies = [
@@ -990,20 +1021,30 @@
             copy.start()
         return copies
 
-    parts = [
-        (in_fin.at[pl.ds(256 * q, 256)], in_out.at[:, pl.ds(256 * q, 256)])
-        for q in range(HID // C)
-    ]
-    copies = move([(out_fin, out_out)] + parts, 0)
+    rest = HID - PLANE_AT
+    parts = [(fin_z, out_out.at[pl.ds(0, PLANE_AT)])]
+    for q in range(1, HID // C):
+        parts.append((fin_y.at[pl.ds(256 * (q - 1), 256)], in_out.at[:, pl.ds(256 * q, 256)]))
+    for half in range(2):
+        cols = pl.ds(128 * half, 128)
+        parts.append((fin_plane.at[half, pl.ds(0, rest)], out_out.at[pl.ds(PLANE_AT, rest), cols]))
+        parts.append((fin_plane.at[half, pl.ds(rest, C)], in_out.at[:, cols]))
+    copies = move(parts, 0)
     kg[...] = small[0:49]
     gain[...] = small[49:50]
     scale[...] = small[50:51]
-    copies += move([(kg, kg_out), (gain, gain_out), (scale, scale_out)], 5)
+    copies += move([(kg, kg_out), (gain, gain_out), (scale, scale_out)], len(parts))
     for copy in copies:
         copy.wait()
 
 
-def hand_over(out_fin, in_fin, small_fin):
+def hand_over(fin_z, fin_plane, fin_y, fin_small):
+    fins = (
+        fin_z.reshape(2 * CROSS, C),
+        fin_plane.reshape(2, 2 * PLANE, 128),
+        fin_y.reshape(2 * CROSS, C),
+        fin_small.reshape(64, C),
+    )
     return pl.pallas_call(
         hand_over_kernel,
         out_shape=(
@@ -1013,20 +1054,16 @@
             jax.ShapeDtypeStruct((C, HID), BF16),
             jax.ShapeDtypeStruct((HID, C), BF16),
         ),
-        in_specs=[pl.BlockSpec(memory_space=pltpu.VMEM)] * 3,
+        in_specs=[pl.BlockSpec(memory_space=pltpu.VMEM)] * 4,
         out_specs=(pl.BlockSpec(memory_space=pl.ANY),) * 5,
         scratch_shapes=[
             pltpu.VMEM((49, C), F32),
             pltpu.VMEM((1, C), F32),
             pltpu.VMEM((1, C), F32),
-            pltpu.SemaphoreType.DMA((8,)),
+            pltpu.SemaphoreType.DMA((11,)),
         ],
         compiler_params=pltpu.CompilerParams(has_side_effects=True),
-    )(
-        pltpu.with_memory_space_constraint(out_fin.reshape(HID, C), pltpu.VMEM),
-        pltpu.with_memory_space_constraint(in_fin.reshape(HID, C), pltpu.VMEM),
-        pltpu.with_memory_space_constraint(small_fin.reshape(64, C), pltpu.VMEM),
-    )
+    )(*[pltpu.with_memory_space_constraint(fin, pltpu.VMEM) for fin in fins])
 
 
 def on_device(state, cotangent, kernel, ln_gain, w_in, w_out, layer_scale, neighbours, codes):

time: 77.4 us -> 72.7 us (0.939)
  Pallas kernels: 76.4 us -> 71.8 us
    pallas_call x1, Pallas kernels: 75.4 us -> 70.7 us  [block_grads(): pl.pallas_call(block_kernel, out_shape=(pltpu.VMEM((2, NZ, CHUNK, C), BF1...]
where the time goes in v4:
time: 72.7 us; the launch traced here: 72.6 us
  Pallas kernels  71.8 us (99%)
  between operations  0.8 us (1%)
    pallas_call x1, Pallas kernels, block_grads(): pl.pallas_call(block_kernel, out_shape=(pltpu.VMEM((2, NZ, CHUNK, C), BF1...  70.7 us

profile of v4, /device:TPU:1, one launch (start us, length us, event | category | flops | bytes accessed | tf_op | source)
XLA Modules:
  0.0 72.6 jit_solution(4034468560427957214)
XLA Ops:
  0.6 70.7 %shard_map.128 = (bf16[2,8,48,256]{3,2,1,0:T(8,128)(2,1)S(1)}, bf16[2,2,4,4,16,128]{5,4,3,2,1,0:T(8,128)(2,1)S(1)}, bf16[2,8,48,256]{3,2,1,0:T(8,128)(2,1)S(1)}, f32[2,4,8,256]{3,2,1,0:T(8,128)S(1)}) custom-call(s32[8,16]{1,0:T(8,128)} %bitcast.18, s32[8,16]{1,0:T(8,128)} %bitcast.19, bf16[32,32,256]{2,1,0:T(8,128)(2,1)} %bitcast.16, ...), custom_call_target="tpu_custom_call" | custom-call | tf_op jit(solution)/shard_map/pallas_call | solution.py:990
  71.4 1.1 %shard_map.129 = (f32[49,256]{1,0:T(8,128)}, f32[1,256]{1,0:T(1,128)}, f32[1,256]{1,0:T(1,128)}, bf16[256,1024]{1,0:T(8,128)(2,1)}, bf16[1024,256]{1,0:T(8,128)(2,1)}) custom-call(bf16[768,256]{1,0:T(8,128)(2,1)S(1)} %bitcast.12, bf16[2,512,128]{2,1,0:T(8,128)(2,1)S(1)} %bitcast.14, bf16[768,256]{1,0:T(8,128)(2,1)S(1)} %bitcast.13, f32[64,256]{1,0:T(8,128)S(1)} %bitcast.15), custom_call_target="tpu_custom_call" | custom-call | tf_op jit(solution)/shard_map/pallas_call | solution.py:1048

commit v5 on v4

--- a/solution.py
+++ b/solution.py
@@ -71,9 +71,14 @@
         self.started.append(copy)
         return copy
 
+    def settle(self, keep):
+        at = len(self.started) - keep
+        for copy in self.started[:at]:
+            copy.wait_send()
+        self.started = self.started[at:]
+
     def finish(self):
-        for copy in self.started:
-            copy.wait_send()
+        self.settle(0)
 
 
 HALF = C // 2
@@ -129,7 +134,7 @@
                 else:
                     piece = self.gath[row, e, :, 0:16, :].astype(F32)
                     for r in range(3):
-                        self.cf[pl.ds(16 * (s - 4) + 4 * r, 4), :] = piece[r, 0:4]
+                        self.cf[pl.ds(12 * (s - 4) + 4 * r, 4), :] = piece[r, 0:4]
             packed = self.cf[...].astype(BF16)
             if k:
                 self.out_c[k - 1] = packed
@@ -148,8 +153,9 @@
             if s < 4:
                 sides[s, :, :, chans] = self.in_s[col, s]
             else:
-                piece = self.in_c[col, pl.ds(16 * (s - 4), 16)]
-                corners[s - 4, :, chans] = jnp.where(n >= 0, piece, jnp.zeros_like(piece))
+                at = 12 * (s - 4)
+                piece = self.in_c[col].astype(F32)[at : at + 12]
+                corners[s - 4, 0:12, chans] = jnp.where(n >= 0, piece, jnp.zeros_like(piece))
 
 
 def both_rims(net, me, ids, codes, along_y, along_x, bufs_y, bufs_x):
@@ -178,10 +184,10 @@
     half = [
         pltpu.VMEM((4, 4, 3, S, HALF), BF16),
         pltpu.VMEM((3, 4, 3, S, HALF), BF16),
-        pltpu.VMEM((3, 64, HALF), BF16),
+        pltpu.VMEM((3, 48, HALF), BF16),
         pltpu.VMEM((4, 4, 3, S, HALF), BF16),
-        pltpu.VMEM((4, 64, HALF), BF16),
-        pltpu.VMEM((64, HALF), F32),
+        pltpu.VMEM((4, 48, HALF), BF16),
+        pltpu.VMEM((48, HALF), F32),
     ]
     return half * 2
 
@@ -218,14 +224,13 @@
     lax.fori_loop(0, S, one_row, 0)
 
 
-def frame_rims(sides, corners, fr, cf, chans):
+def frame_rims(sides, cf, fr, chans):
     turn = reversal()
     for r in range(3):
         fr[r, 3 : 3 + S, chans] = flip(turn, sides[0, 2 - r, :, chans]).astype(F32)
         fr[3 : 3 + S, 35 + r, chans] = flip(turn, sides[1, r, :, chans]).astype(F32)
         fr[35 + r, 3 : 3 + S, chans] = sides[2, r, :, chans].astype(F32)
         fr[3 : 3 + S, r, chans] = sides[3, 2 - r, :, chans].astype(F32)
-    cf[:, :, chans] = corners[:, :, chans].astype(F32)
     for i in range(3):
         for j in range(3):
             fr[i, j, chans] = cf[0, 4 * (2 - i) + 2 - j, chans]
@@ -240,7 +245,7 @@
             fb[b, first + i, :, chans] = fr[first + i, b : b + S, chans]
         return carry
 
-    lax.fori_loop(0, count, one_row, 0)
+    lax.fori_loop(0, count, one_row, 0, unroll=3 if count % 3 == 0 else 4)
 
 
 def shift_sides(fr, fs, chans):
@@ -252,7 +257,7 @@
             fs[b, i, 3:6, chans] = fr[3 + i, 29 + b : 32 + b, chans]
         return carry
 
-    lax.fori_loop(0, S, one_row, 0)
+    lax.fori_loop(0, S, one_row, 0, unroll=4)
 
 
 def lanes(g):
@@ -311,9 +316,10 @@
     square = v * v
     inner = v * (root + (root * 0.044715) * square)
     t = jnp.tanh(inner)
-    half = 0.5 * (1.0 + t)
-    slope = half + (0.5 * v) * (1.0 - t * t) * (root + (3.0 * root * 0.044715) * square)
-    return v * half, slope
+    half = 0.5 + 0.5 * t
+    value = v * half
+    slope = half + value * (1.0 - half) * (2.0 * root + (6.0 * root * 0.044715) * square)
+    return value, slope
 
 
 def dot(left, right):
@@ -839,6 +845,7 @@
     by_z.over_x()
     by_y.over_x()
     smalls.over_y()
+    smalls.net.settle(20)
     plane.over_z()
     by_z.over_other()
     by_y.over_other()
@@ -848,9 +855,11 @@
     by_y.back_first()
     smalls.back_x()
     plane.back_x()
+    smalls.net.settle(30)
     by_z.back_core()
     smalls.back_core()
     by_y.back_core()
+    smalls.net.settle(12)
     plane.back_core()
     smalls.finish()
     by_z.finish()
@@ -868,7 +877,6 @@
         pltpu.VMEM((7, ROWS, S, C), F32),
         pltpu.VMEM((7, S, 8, C), F32),
         pltpu.VMEM((4, 3, S, C), BF16),
-        pltpu.VMEM((4, 16, C), BF16),
         pltpu.VMEM((4, 16, C), F32),
         pltpu.VMEM((C, HID), F32),
         pltpu.VMEM((C, HID), F32),
@@ -896,7 +904,7 @@
         rest, shared_scratch(), weight_scratch(), rim_scratch(), inside_scratch(),
         border_scratch(), sum_scratch(),
     )
-    ids, codes, xb, xf, fr, fb, fs, sides, corners, cf, gacc, iacc, kg, gain_acc, big, small = shared
+    ids, codes, xb, xf, fr, fb, fs, sides, corners, gacc, iacc, kg, gain_acc, big, small = shared
     ss, rs, ls = sems
     w = Weights(weights)
     me = Place()
@@ -953,7 +961,7 @@
 
     for rim, chans in ((by_y, slice(0, HALF)), (by_x, slice(HALF, C))):
         rim.take(sides, corners, chans, me.space)
-        frame_rims(sides, corners, fr, cf, chans)
+        frame_rims(sides, corners, fr, chans)
         shift_rows(fr, fb, 0, 9, chans)
         shift_rows(fr, fb, S - 3, 9, chans)
         shift_sides(fr, fs, chans)

time: 72.7 us -> 71.9 us (0.989)
  no operation moved by 1% of the time
where the time goes in v5:
time: 71.9 us
  Pallas kernels  71.1 us (99%)
  between operations  0.8 us (1%)
    pallas_call x1, Pallas kernels, block_grads(): pl.pallas_call(block_kernel, out_shape=(pltpu.VMEM((2, NZ, CHUNK, C), BF1...  70 us

profile of v5, /device:TPU:1, one launch (start us, length us, event | category | flops | bytes accessed | tf_op | source)
XLA Modules:
  0.0 71.9 jit_solution(4010831666877722261)
XLA Ops:
  0.6 70.0 %shard_map.128 = (bf16[2,8,48,256]{3,2,1,0:T(8,128)(2,1)S(1)}, bf16[2,2,4,4,16,128]{5,4,3,2,1,0:T(8,128)(2,1)S(1)}, bf16[2,8,48,256]{3,2,1,0:T(8,128)(2,1)S(1)}, f32[2,4,8,256]{3,2,1,0:T(8,128)S(1)}) custom-call(s32[8,16]{1,0:T(8,128)} %bitcast.18, s32[8,16]{1,0:T(8,128)} %bitcast.19, bf16[32,32,256]{2,1,0:T(8,128)(2,1)} %bitcast.16, ...), custom_call_target="tpu_custom_call" | custom-call | tf_op jit(solution)/shard_map/pallas_call | solution.py:998
  70.7 1.1 %shard_map.129 = (f32[49,256]{1,0:T(8,128)}, f32[1,256]{1,0:T(1,128)}, f32[1,256]{1,0:T(1,128)}, bf16[256,1024]{1,0:T(8,128)(2,1)}, bf16[1024,256]{1,0:T(8,128)(2,1)}) custom-call(bf16[768,256]{1,0:T(8,128)(2,1)S(1)} %bitcast.12, bf16[2,512,128]{2,1,0:T(8,128)(2,1)S(1)} %bitcast.14, bf16[768,256]{1,0:T(8,128)(2,1)S(1)} %bitcast.13, f32[64,256]{1,0:T(8,128)S(1)} %bitcast.15), custom_call_target="tpu_custom_call" | custom-call | tf_op jit(solution)/shard_map/pallas_call | solution.py:1056

commit v6 on v5

--- a/solution.py
+++ b/solution.py
@@ -977,8 +977,8 @@
     border.in_grad(iacc, big)
     plane.start()
     sum_y.start()
+    sum_z.over_first()
     border.scaled_grad()
-    sum_z.over_first()
     plane.over_x()
     sum_y.over_first()
     gain = border.backward(gain_acc)

time: 71.9 us -> 72.3 us (level)
  no operation moved by 1% of the time
where the time goes in v6:
time: 72.3 us; the launch traced here: 72.1 us
  Pallas kernels  71.3 us (99%)
  between operations  0.8 us (1%)
    pallas_call x1, Pallas kernels, block_grads(): pl.pallas_call(block_kernel, out_shape=(pltpu.VMEM((2, NZ, CHUNK, C), BF1...  70.2 us

profile of v6, /device:TPU:1, one launch (start us, length us, event | category | flops | bytes accessed | tf_op | source)
XLA Modules:
  0.0 72.1 jit_solution(2414260250902423961)
XLA Ops:
  0.6 70.2 %shard_map.128 = (bf16[2,8,48,256]{3,2,1,0:T(8,128)(2,1)S(1)}, bf16[2,2,4,4,16,128]{5,4,3,2,1,0:T(8,128)(2,1)S(1)}, bf16[2,8,48,256]{3,2,1,0:T(8,128)(2,1)S(1)}, f32[2,4,8,256]{3,2,1,0:T(8,128)S(1)}) custom-call(s32[8,16]{1,0:T(8,128)} %bitcast.18, s32[8,16]{1,0:T(8,128)} %bitcast.19, bf16[32,32,256]{2,1,0:T(8,128)(2,1)} %bitcast.16, ...), custom_call_target="tpu_custom_call" | custom-call | tf_op jit(solution)/shard_map/pallas_call | solution.py:998
  70.9 1.1 %shard_map.129 = (f32[49,256]{1,0:T(8,128)}, f32[1,256]{1,0:T(1,128)}, f32[1,256]{1,0:T(1,128)}, bf16[256,1024]{1,0:T(8,128)(2,1)}, bf16[1024,256]{1,0:T(8,128)(2,1)}) custom-call(bf16[768,256]{1,0:T(8,128)(2,1)S(1)} %bitcast.12, bf16[2,512,128]{2,1,0:T(8,128)(2,1)S(1)} %bitcast.14, bf16[768,256]{1,0:T(8,128)(2,1)S(1)} %bitcast.13, f32[64,256]{1,0:T(8,128)S(1)} %bitcast.15), custom_call_target="tpu_custom_call" | custom-call | tf_op jit(solution)/shard_map/pallas_call | solution.py:1056
